TPU v7x, 32 devices: a whole 2x2x4 slice. The times are simulated.
32 devices in a mesh: seq: 16 (over z, y, x), head: 2 (over core).
Axes of the slice: x: 2, y: 2, z: 4, core: 2. Of those that a mesh axis runs over, the one named last changes fastest.
Arguments:
- queries: bfloat16 [4096, 2048], P('seq', 'head'), may hold values from -4 to 4
- first_pair_keys: bfloat16 [4096, 1024], P('seq', 'head'), may hold values from -4 to 4
- first_pair_values: bfloat16 [4096, 1024], P('seq', 'head'), may hold values from -6 to 6
- second_pair_keys: bfloat16 [4096, 1024], P('seq', 'head'), may hold values from -4 to 4
- second_pair_values: bfloat16 [4096, 1024], P('seq', 'head'), may hold values from -6 to 6
- out_weight: bfloat16 [2048, 8192], P('seq', 'head'), may hold values from -0.125 to 0.125
Outputs:
- attended: bfloat16 [4096, 2048], P('seq', 'head')
- projected: bfloat16 [4096, 8192], P('seq', 'head')
All inputs are finite; a program needn't handle non-finite values.
Results may differ from a plain program's by a relative error of at most 0.0064.
Values may be sent and summed in bfloat16 or wider, within the bound.
A program may use at most 192 MiB of HBM per device.

v0:
```python
import math

import jax
import jax.numpy as jnp
from jax import lax
from jax.sharding import PartitionSpec as P

HEAD_SIZE = 128
GROUP_QUERIES = 2
FIRST_WINDOW = 512
SECOND_WINDOW = 32


def passed_along(x, axis, by):
    size = lax.axis_size(axis)
    pairs = [(i, i + by) for i in range(size) if 0 <= i + by < size]
    return lax.ppermute(x, axis, pairs)


def attend_block(query_rows, first_rows, first_vals, second_win, second_vwin, query_pos, key_pos):
    score_scale = HEAD_SIZE ** (-0.5)
    query_mod = (
        query_rows.astype(jnp.float32)[:, None] * second_win.astype(jnp.float32)[:, :, :, None, :]
    ).astype(jnp.bfloat16)
    scores = (
        jnp.einsum("itvgd,jvd->ivgtj", query_mod, first_rows, preferred_element_type=jnp.float32)
        * score_scale
    )
    key_lag = query_pos[:, None] - key_pos[None, :]
    first_ok = (key_lag >= 0) & (key_lag < FIRST_WINDOW) & (key_pos[None, :] >= 0)
    offsets = jnp.arange(SECOND_WINDOW, dtype=jnp.int32)
    second_ok = query_pos[:, None] - offsets[None, :] >= 0
    is_valid = first_ok[:, None, None, None, :] & second_ok[:, None, None, :, None]
    scores = jnp.where(is_valid, scores, -jnp.inf)
    row_top = jnp.max(scores, axis=(3, 4), keepdims=True)
    row_weights = jnp.exp(scores - row_top)
    row_sum = jnp.sum(row_weights, axis=(3, 4))
    weights_bf = row_weights.astype(jnp.bfloat16)
    first_mix = jnp.einsum(
        "ivgtj,jvd->ivgtd", weights_bf, first_vals, preferred_element_type=jnp.float32
    )
    second_side = jnp.transpose(second_vwin, (0, 2, 1, 3)).astype(jnp.float32)[:, :, None]
    combined = jnp.sum(first_mix * second_side, axis=3)
    return (combined / row_sum[..., None]).astype(jnp.bfloat16)


def on_device(
    queries, first_pair_keys, first_pair_values, second_pair_keys, second_pair_values, out_weight
):
    local_rows = queries.shape[0]
    kv_local = first_pair_keys.shape[1] // HEAD_SIZE
    seq_index = lax.axis_index("seq")
    hop_count = FIRST_WINDOW // local_rows
    key_pair = jnp.stack([first_pair_keys, first_pair_values])
    earlier = []
    moving = key_pair
    for hop_step in range(hop_count):
        moving = passed_along(moving, "seq", 1)
        earlier.insert(0, moving)
    window_pair = jnp.concatenate(earlier + [key_pair], axis=1)
    tail_start = local_rows - SECOND_WINDOW + 1
    edge_pair = passed_along(
        jnp.stack([second_pair_keys[tail_start:], second_pair_values[tail_start:]]), "seq", 1
    )
    near_pair = jnp.concatenate(
        [edge_pair, jnp.stack([second_pair_keys, second_pair_values])], axis=1
    )
    window_keys = window_pair[0].reshape(-1, kv_local, HEAD_SIZE)
    window_values = window_pair[1].reshape(-1, kv_local, HEAD_SIZE)
    near_keys = near_pair[0].reshape(-1, kv_local, HEAD_SIZE)
    near_values = near_pair[1].reshape(-1, kv_local, HEAD_SIZE)
    query_head_count = queries.reshape(local_rows, kv_local, GROUP_QUERIES, HEAD_SIZE)
    block_rows = math.gcd(64, local_rows)
    outputs = []
    for block_index in range(local_rows // block_rows):
        block_start = block_index * block_rows
        query_rows = query_head_count[block_start : block_start + block_rows]
        first_rows = window_keys[block_start : block_start + block_rows + FIRST_WINDOW]
        first_vals = window_values[block_start : block_start + block_rows + FIRST_WINDOW]
        near_k = near_keys[block_start : block_start + block_rows + SECOND_WINDOW - 1]
        near_v = near_values[block_start : block_start + block_rows + SECOND_WINDOW - 1]
        second_win = jnp.stack(
            [
                near_k[SECOND_WINDOW - 1 - lag_step : SECOND_WINDOW - 1 - lag_step + block_rows]
                for lag_step in range(SECOND_WINDOW)
            ],
            axis=1,
        )
        second_vwin = jnp.stack(
            [
                near_v[SECOND_WINDOW - 1 - lag_step : SECOND_WINDOW - 1 - lag_step + block_rows]
                for lag_step in range(SECOND_WINDOW)
            ],
            axis=1,
        )
        query_first = seq_index * local_rows + block_start
        query_pos = query_first + jnp.arange(block_rows, dtype=jnp.int32)
        key_pos = (
            query_first - FIRST_WINDOW + jnp.arange(block_rows + FIRST_WINDOW, dtype=jnp.int32)
        )
        outputs.append(
            attend_block(
                query_rows, first_rows, first_vals, second_win, second_vwin, query_pos, key_pos
            )
        )
    attended = jnp.concatenate(outputs, axis=0).reshape(
        local_rows, kv_local * GROUP_QUERIES * HEAD_SIZE
    )
    all_heads = lax.all_gather(attended, "head", axis=1, tiled=True)
    projected = jnp.dot(
        all_heads,
        lax.all_gather(out_weight, "seq", axis=0, tiled=True),
        preferred_element_type=jnp.float32,
    )
    return (attended, projected.astype(jnp.bfloat16))


def solution(mesh):
    return jax.shard_map(
        on_device,
        mesh=mesh,
        in_specs=(
            P("seq", "head"),
            P("seq", "head"),
            P("seq", "head"),
            P("seq", "head"),
            P("seq", "head"),
            P("seq", "head"),
        ),
        out_specs=(P("seq", "head"), P("seq", "head")),
        check_vma=False,
    )
```

profile of v0, /device:TPU:0, one launch (start us, length us, event | category | flops | bytes accessed | tf_op | source)
XLA Modules:
  0.0 930.3 jit_solution(7732470468926434826)
XLA Ops:
  7.2 1.9 pad_maximum_fusion
  9.1 5.6 collective-permute-start
  16.2 3.2 collective-permute-start.2
  38.5 1.5 stack.1060
  47.3 1.5 stack.1066
  66.5 1.5 stack.1079
  69.5 1.5 stack.1081
  98.9 2.5 convert_bitcast_fusion
  117.0 1.5 stack.1003
  133.2 1.5 stack.1014
  146.5 1.5 stack.1023
  164.1 2.5 convert_bitcast_fusion.1
  170.4 1.5 stack.929
  174.9 1.5 stack.932
  185.2 1.5 stack.939
  200.0 1.5 stack.949
  227.7 2.5 convert_bitcast_fusion.2
  230.4 1.8 broadcast_and_fusion
  232.4 1.7 broadcast_and_fusion.1
  234.3 1.6 broadcast_and_fusion.2
  236.1 1.6 broadcast_and_fusion.3
  259.8 12.0 %stack.1058 = bf16[64,32,4,128]{3,1,2,0:T(8,128)(2,1)S(1)} concatenate(bf16[64,1,4,128]{3,1,2,0:T(2,128)(2,1)S(1)} %stack.1188, bf16[64,1,4,128]{3,1,2,0:T(2,128)(2,1)} %stack.1189, bf16[64,1,4,128]{3,1,2,0:T(2,128)(2,1)} %stack.1190, bf16[64,1,4,128]{3,1,2,0:T(2,128)(2,1)} %stack.1191, bf16[64,1,4,128]{3,1,2,0:T(2,128)(2,1)} %stack.1192, bf16[64,1,4,128]{3,1,2,0:T(2,128)(2,1)} %stack.1193, ...), dimensions={1} | concatenate | bytes 4194304 | tf_op jit(solution)/shard_map/stack | solution.py:82
  271.8 3.3 copy.991
  278.1 1.6 stack.1157
  279.7 1.5 stack.1158
  281.2 1.5 stack.1159
  282.8 1.6 stack.1160
  284.3 1.5 stack.1161
  303.8 12.2 %stack.992 = bf16[64,32,4,128]{3,1,2,0:T(8,128)(2,1)S(1)} concatenate(bf16[64,1,4,128]{3,1,2,0:T(2,128)(2,1)S(1)} %stack.1156, bf16[64,1,4,128]{3,1,2,0:T(2,128)(2,1)} %stack.1157, bf16[64,1,4,128]{3,1,2,0:T(2,128)(2,1)} %stack.1158, bf16[64,1,4,128]{3,1,2,0:T(2,128)(2,1)} %stack.1159, bf16[64,1,4,128]{3,1,2,0:T(2,128)(2,1)} %stack.1160, bf16[64,1,4,128]{3,1,2,0:T(2,128)(2,1)} %stack.1161, ...), dimensions={1} | concatenate | bytes 4194304 | tf_op jit(solution)/shard_map/stack | solution.py:82
  316.0 3.4 copy.921
  321.5 1.6 stack.1128
  323.1 1.5 stack.1129
  324.6 1.5 stack.1130
  344.1 11.9 %stack.926 = bf16[64,32,4,128]{3,1,2,0:T(8,128)(2,1)S(1)} concatenate(bf16[64,1,4,128]{3,1,2,0:T(2,128)(2,1)} %stack.1124, bf16[64,1,4,128]{3,1,2,0:T(2,128)(2,1)S(1)} %stack.1125, bf16[64,1,4,128]{3,1,2,0:T(2,128)(2,1)S(1)} %stack.1126, bf16[64,1,4,128]{3,1,2,0:T(2,128)(2,1)S(1)} %stack.1127, bf16[64,1,4,128]{3,1,2,0:T(2,128)(2,1)} %stack.1128, ...), dimensions={1} | concatenate | bytes 4194304 | tf_op jit(solution)/shard_map/stack | solution.py:82
  356.0 3.2 copy.851
  365.6 1.5 stack.863
  377.5 1.5 stack.875
  379.4 1.5 constant_dynamic-update-slice_fusion.30
  418.9 11.0 %stack.860 = bf16[64,32,4,128]{3,1,2,0:T(8,128)(2,1)S(1)} concatenate(bf16[64,1,4,128]{3,1,2,0:T(2,128)(2,1)S(1)} %stack.1092, bf16[64,1,4,128]{3,1,2,0:T(2,128)(2,1)} %stack.1093, bf16[64,1,4,128]{3,1,2,0:T(2,128)(2,1)} %stack.1094, bf16[64,1,4,128]{3,1,2,0:T(2,128)(2,1)} %stack.1095, bf16[64,1,4,128]{3,1,2,0:T(2,128)(2,1)} %stack.1096, bf16[64,1,4,128]{3,1,2,0:T(2,128)(2,1)} %stack.1097, ...), dimensions={1} | concatenate | bytes 4194304 | tf_op jit(solution)/shard_map/stack | solution.py:82
  429.9 3.3 copy.781
  434.6 2.8 collective-permute-start.1
  438.1 4.1 convert_bitcast_fusion.3
  442.2 6.1 collective-permute-done.1
  449.4 1.7 fusion.60
  451.1 2.4 slice.1620
  453.5 2.3 slice.1618
  455.9 19.1 %fusion.11 = (f32[64,4,2]{0,2,1:T(2,128)S(1)}, f32[4,576,64,32,2]{1,2,4,3,0:T(8,128)}) fusion(pred[64,32,576]{2,0,1:T(8,128)(4,1)S(1)} %copy-done.5, f32[64,32,4,128]{3,0,1,2:T(8,128)} %copy.991, f32[64,4,2,128]{3,0,2,1:T(8,128)S(1)} %copy-done.99, bf16[576,4,128,1,1]{2,1,0,4,3:T(4,128)(2,1)} %bitcast.97), kind=kOutput, calls=%fused_computation.19 | convolution fusion | flops 2448424448 | bytes 43976704 | tf_op jit(solution)/shard_map/itvgd,jvd->ivgtj/dot_general | solution.py:26
  474.9 28.5 %fusion.6 = (f32[64,4,2]{0,2,1:T(2,128)S(1)}, bf16[64,4,2,32,576]{4,0,2,3,1:T(8,128)(2,1)}) fusion(f32[4,576,64,32,2]{1,2,4,3,0:T(8,128)} %get-tuple-element.285, f32[64,4,2]{0,2,1:T(2,128)S(1)} %get-tuple-element.284, pred[64,32,576]{2,0,1:T(8,128)(4,1)S(1)} %copy-done.5), kind=kLoop, calls=%fused_computation.14 | loop fusion | flops 47185408 | bytes 57806848 | tf_op jit(solution)/shard_map/reduce_sum | solution.py:37
  503.5 11.3 %fusion.20 = f32[64,4,2,128]{3,0,2,1:T(8,128)S(1)} fusion(f32[64,4,32,128]{3,0,2,1:T(8,128)} %convert_bitcast_fusion, bf16[64,4,2,32,576]{4,0,2,3,1:T(8,128)(2,1)} %get-tuple-element.3, bf16[576,4,128,1,1]{2,1,0,4,3:T(4,128)(2,1)} %bitcast.92), kind=kOutput, calls=%fused_computation.29 | convolution fusion | flops 2420047872 | bytes 23920640 | tf_op jit(solution)/shard_map/ivgtj,jvd->ivgtd/dot_general | solution.py:39
  515.2 2.3 slice.1551
  517.5 2.3 slice.1549
  519.8 19.3 %fusion.10 = (f32[64,4,2]{0,2,1:T(2,128)S(1)}, f32[4,576,64,32,2]{1,2,4,3,0:T(8,128)}) fusion(pred[64,32,576]{2,0,1:T(8,128)(4,1)S(1)} %copy-done.4, f32[64,32,4,128]{3,0,1,2:T(8,128)} %copy.921, f32[64,4,2,128]{3,0,2,1:T(8,128)S(1)} %copy-done.100, bf16[576,4,128,1,1]{2,1,0,4,3:T(4,128)(2,1)} %bitcast.98), kind=kOutput, calls=%fused_computation.18 | convolution fusion | flops 2448424448 | bytes 43976704 | tf_op jit(solution)/shard_map/itvgd,jvd->ivgtj/dot_general | solution.py:26
  539.1 28.5 %fusion.4 = (f32[64,4,2]{0,2,1:T(2,128)S(1)}, bf16[64,4,2,32,576]{4,0,2,3,1:T(8,128)(2,1)}) fusion(f32[4,576,64,32,2]{1,2,4,3,0:T(8,128)} %get-tuple-element.283, f32[64,4,2]{0,2,1:T(2,128)S(1)} %get-tuple-element.282, pred[64,32,576]{2,0,1:T(8,128)(4,1)S(1)} %copy-done.4), kind=kLoop, calls=%fused_computation.12 | loop fusion | flops 47185408 | bytes 57806848 | tf_op jit(solution)/shard_map/reduce_sum | solution.py:37
  567.6 11.3 %fusion.21 = f32[64,4,2,128]{3,0,2,1:T(8,128)S(1)} fusion(f32[64,4,32,128]{3,0,2,1:T(8,128)} %convert_bitcast_fusion.1, bf16[64,4,2,32,576]{4,0,2,3,1:T(8,128)(2,1)} %get-tuple-element.5, bf16[576,4,128,1,1]{2,1,0,4,3:T(4,128)(2,1)} %bitcast.93), kind=kOutput, calls=%fused_computation.31 | convolution fusion | flops 2420047872 | bytes 23920640 | tf_op jit(solution)/shard_map/ivgtj,jvd->ivgtd/dot_general | solution.py:39
  579.3 2.3 slice.1482
  582.6 19.3 %fusion.9 = (f32[64,4,2]{0,2,1:T(2,128)S(1)}, f32[4,576,64,32,2]{1,2,4,3,0:T(8,128)}) fusion(pred[64,32,576]{2,0,1:T(8,128)(4,1)S(1)} %copy-done.3, f32[64,32,4,128]{3,0,1,2:T(8,128)} %copy.851, f32[64,4,2,128]{3,0,2,1:T(8,128)} %copy.818, bf16[576,4,128,1,1]{2,1,0,4,3:T(4,128)(2,1)} %bitcast.99), kind=kOutput, calls=%fused_computation.17 | convolution fusion | flops 2448424448 | bytes 43976704 | tf_op jit(solution)/shard_map/itvgd,jvd->ivgtj/dot_general | solution.py:26
  601.9 28.6 %fusion.2 = (f32[64,4,2]{0,2,1:T(2,128)S(1)}, bf16[64,4,2,32,576]{4,0,2,3,1:T(8,128)(2,1)}) fusion(f32[4,576,64,32,2]{1,2,4,3,0:T(8,128)} %get-tuple-element.281, f32[64,4,2]{0,2,1:T(2,128)S(1)} %get-tuple-element.280, pred[64,32,576]{2,0,1:T(8,128)(4,1)S(1)} %copy-done.3), kind=kLoop, calls=%fused_computation.10 | loop fusion | flops 47185408 | bytes 57806848 | tf_op jit(solution)/shard_map/reduce_sum | solution.py:37
  630.5 11.9 %fusion.22 = f32[64,4,2,128]{3,0,2,1:T(8,128)} fusion(f32[64,4,32,128]{3,0,2,1:T(8,128)} %convert_bitcast_fusion.2, bf16[64,4,2,32,576]{4,0,2,3,1:T(8,128)(2,1)} %get-tuple-element.7, bf16[576,4,128,1,1]{2,1,0,4,3:T(4,128)(2,1)S(1)} %bitcast.94), kind=kOutput, calls=%fused_computation.33 | convolution fusion | flops 2420047872 | bytes 23920640 | tf_op jit(solution)/shard_map/ivgtj,jvd->ivgtd/dot_general | solution.py:39
  644.1 19.1 %fusion.8 = (f32[64,4,2]{0,2,1:T(2,128)S(1)}, f32[4,576,64,32,2]{1,2,4,3,0:T(8,128)}) fusion(pred[64,32,576]{2,0,1:T(8,128)(4,1)S(1)} %copy-done.2, f32[64,32,4,128]{3,0,1,2:T(8,128)} %copy.781, f32[64,4,2,128]{3,0,2,1:T(8,128)} %copy.748, bf16[576,4,128,1,1]{2,1,0,4,3:T(4,128)(2,1)S(1)} %bitcast.96), kind=kOutput, calls=%fused_computation.16 | convolution fusion | flops 2448424448 | bytes 43976704 | tf_op jit(solution)/shard_map/itvgd,jvd->ivgtj/dot_general | solution.py:26
  663.2 28.5 %fusion = (f32[64,4,2]{0,2,1:T(2,128)S(1)}, bf16[64,4,2,32,576]{4,0,2,3,1:T(8,128)(2,1)}) fusion(f32[4,576,64,32,2]{1,2,4,3,0:T(8,128)} %get-tuple-element.279, f32[64,4,2]{0,2,1:T(2,128)S(1)} %get-tuple-element.278, pred[64,32,576]{2,0,1:T(8,128)(4,1)S(1)} %copy-done.2), kind=kLoop, calls=%fused_computation.8 | loop fusion | flops 47185408 | bytes 57806848 | tf_op jit(solution)/shard_map/reduce_sum | solution.py:37
  691.7 11.2 %fusion.23 = f32[64,4,2,128]{3,0,2,1:T(8,128)S(1)} fusion(f32[64,4,32,128]{3,0,2,1:T(8,128)} %convert_bitcast_fusion.3, bf16[64,4,2,32,576]{4,0,2,3,1:T(8,128)(2,1)} %get-tuple-element.9, bf16[576,4,128,1,1]{2,1,0,4,3:T(4,128)(2,1)S(1)} %bitcast.95), kind=kOutput, calls=%fused_computation.35 | convolution fusion | flops 2420047872 | bytes 23920640 | tf_op jit(solution)/shard_map/ivgtj,jvd->ivgtd/dot_general | solution.py:39
  704.9 10.5 %all-gather.3.cloned.1.call-done = bf16[256,2048]{1,0:T(8,128)(2,1)} async-done(((bf16[256,1024]{1,0:T(8,128)(2,1)}), bf16[256,2048]{1,0:T(8,128)(2,1)}) %all-gather.3.cloned.1.call-update) | async-done | bytes 1048592 | tf_op jit(solution)/shard_map/all_gather | solution.py:109
  715.4 195.6 %all-gather.5.cloned.1.call-done = bf16[2048,4096]{1,0:T(8,128)(2,1)} async-done(((bf16[128,4096]{1,0:T(8,128)(2,1)}), bf16[2048,4096]{1,0:T(8,128)(2,1)}) %all-gather.5.cloned.1.call-update) | async-done | bytes 16777232 | tf_op jit(solution)/shard_map/all_gather | solution.py:112
  911.0 11.9 %convolution_convert_fusion = bf16[256,4096]{1,0:T(8,128)(2,1)} fusion(bf16[256,2048]{1,0:T(8,128)(2,1)} %all-gather.3.cloned.1.call-done, bf16[2048,4096]{1,0:T(8,128)(2,1)} %all-gather.5.cloned.1.call-done), kind=kOutput, calls=%fused_computation.40 | convolution fusion | flops 4296015872 | bytes 19922944 | tf_op jit(solution)/shard_map/dot_general | solution.py:110
  (774 shorter events, 314.2 us)
Async XLA Ops:
  7.2 708.3 %all-gather.3.cloned.1.call-start = ((), (), s32[]{:S(2)}) async-start(), calls=%async_computation | async-start | bytes 1572864 | tf_op jit(solution)/shard_map/all_gather | solution.py:109
  9.1 425.4 %collective-permute-start = (bf16[2,256,512]{2,1,0:T(8,128)(2,1)}, bf16[2,256,512]{2,1,0:T(8,128)(2,1)}, u32[]{:S(2)}, u32[]{:S(2)}) collective-permute-start(bf16[2,256,512]{2,1,0:T(8,128)(2,1)} %pad_maximum_fusion), channel_id=1, source_target_pairs={{0,2},{2,4},{4,6},{6,8},{8,10},{10,12},{12,14},{14,16},{16,18},{18... | collective-permute-start | bytes 1572872 | tf_op jit(solution)/shard_map/ppermute | solution.py:17
  16.2 345.0 %collective-permute-start.2 = (bf16[2,31,512]{2,1,0:T(8,128)(2,1)}, bf16[2,31,512]{2,1,0:T(8,128)(2,1)}, u32[]{:S(2)}, u32[]{:S(2)}) collective-permute-start(bf16[2,31,512]{2,1,0:T(8,128)(2,1)} %pad_maximum_fusion.1), channel_id=1, source_target_pairs={{0,2},{2,4},{4,6},{6,8},{8,10},{10,12},{12,14},{14,16},{16,18},{18... | collective-permute-start | bytes 190472 | tf_op jit(solution)/shard_map/ppermute | solution.py:17
  36.1 28.9 %copy-start.159 = (s32[64]{0:T(128)}, s32[64]{0:T(128)S(1)}, u32[]{:S(2)}) copy-start(s32[64]{0:T(128)S(1)} %iota_add_fusion.4) | copy-start | bytes 772
  84.3 14.4 %copy-start.112 = (bf16[64,1,4,128]{3,2,0,1:T(4,128)(2,1)S(1)}, bf16[64,1,4,128]{3,2,0,1:T(4,128)(2,1)}, u32[]{:S(2)}) copy-start(bf16[64,1,4,128]{3,2,0,1:T(4,128)(2,1)} %stack.1087) | copy-start | bytes 196612
  84.4 14.4 %copy-start.109 = (bf16[64,1,4,128]{3,2,0,1:T(4,128)(2,1)S(1)}, bf16[64,1,4,128]{3,2,0,1:T(4,128)(2,1)}, u32[]{:S(2)}) copy-start(bf16[64,1,4,128]{3,2,0,1:T(4,128)(2,1)} %stack.1088) | copy-start | bytes 196612
  84.4 14.4 %copy-start.103 = (bf16[64,1,4,128]{3,2,0,1:T(4,128)(2,1)S(1)}, bf16[64,1,4,128]{3,2,0,1:T(4,128)(2,1)}, u32[]{:S(2)}) copy-start(bf16[64,1,4,128]{3,2,0,1:T(4,128)(2,1)} %stack.1089) | copy-start | bytes 196612
  84.4 14.5 %copy-start.104 = (bf16[64,1,4,128]{3,2,0,1:T(4,128)(2,1)S(1)}, bf16[64,1,4,128]{3,2,0,1:T(4,128)(2,1)}, u32[]{:S(2)}) copy-start(bf16[64,1,4,128]{3,2,0,1:T(4,128)(2,1)} %stack.1090) | copy-start | bytes 196612
  101.3 46.7 %copy-start.161 = (s32[64]{0:T(128)}, s32[64]{0:T(128)S(1)}, u32[]{:S(2)}) copy-start(s32[64]{0:T(128)S(1)} %iota_add_fusion.5) | copy-start | bytes 772
  149.6 14.4 %copy-start.110 = (bf16[64,1,4,128]{3,2,0,1:T(4,128)(2,1)S(1)}, bf16[64,1,4,128]{3,2,0,1:T(4,128)(2,1)}, u32[]{:S(2)}) copy-start(bf16[64,1,4,128]{3,2,0,1:T(4,128)(2,1)} %stack.1022) | copy-start | bytes 196612
  149.6 14.4 %copy-start.105 = (bf16[64,1,4,128]{3,2,0,1:T(4,128)(2,1)S(1)}, bf16[64,1,4,128]{3,2,0,1:T(4,128)(2,1)}, u32[]{:S(2)}) copy-start(bf16[64,1,4,128]{3,2,0,1:T(4,128)(2,1)} %stack.1023) | copy-start | bytes 196612
  149.6 14.5 %copy-start.106 = (bf16[64,1,4,128]{3,2,0,1:T(4,128)(2,1)S(1)}, bf16[64,1,4,128]{3,2,0,1:T(4,128)(2,1)}, u32[]{:S(2)}) copy-start(bf16[64,1,4,128]{3,2,0,1:T(4,128)(2,1)} %stack.1024) | copy-start | bytes 196612
  212.4 15.2 %copy-start.107 = (bf16[64,1,4,128]{3,2,0,1:T(4,128)(2,1)S(1)}, bf16[64,1,4,128]{3,2,0,1:T(4,128)(2,1)}, u32[]{:S(2)}) copy-start(bf16[64,1,4,128]{3,2,0,1:T(4,128)(2,1)} %stack.957) | copy-start | bytes 196612
  213.2 14.4 %copy-start.111 = (bf16[64,1,4,128]{3,2,0,1:T(4,128)(2,1)S(1)}, bf16[64,1,4,128]{3,2,0,1:T(4,128)(2,1)}, u32[]{:S(2)}) copy-start(bf16[64,1,4,128]{3,2,0,1:T(4,128)(2,1)} %stack.956) | copy-start | bytes 196612
  213.2 14.5 %copy-start.108 = (bf16[64,1,4,128]{3,2,0,1:T(4,128)(2,1)S(1)}, bf16[64,1,4,128]{3,2,0,1:T(4,128)(2,1)}, u32[]{:S(2)}) copy-start(bf16[64,1,4,128]{3,2,0,1:T(4,128)(2,1)} %stack.958) | copy-start | bytes 196612
  238.4 14.4 %copy-start.57 = (bf16[1,64,512]{2,1,0:T(8,128)(2,1)S(1)}, bf16[1,64,512]{2,1,0:T(8,128)(2,1)}, u32[]{:S(2)}) copy-start(bf16[1,64,512]{2,1,0:T(8,128)(2,1)} %get-tuple-element.93) | copy-start | bytes 196612
  239.1 14.4 %copy-start.55 = (bf16[1,64,512]{2,1,0:T(8,128)(2,1)S(1)}, bf16[1,64,512]{2,1,0:T(8,128)(2,1)}, u32[]{:S(2)}) copy-start(bf16[1,64,512]{2,1,0:T(8,128)(2,1)} %get-tuple-element.92) | copy-start | bytes 196612
  239.8 14.4 %copy-start.53 = (bf16[1,64,512]{2,1,0:T(8,128)(2,1)S(1)}, bf16[1,64,512]{2,1,0:T(8,128)(2,1)}, u32[]{:S(2)}) copy-start(bf16[1,64,512]{2,1,0:T(8,128)(2,1)} %get-tuple-element.91) | copy-start | bytes 196612
  240.5 14.4 %copy-start.51 = (bf16[1,64,512]{2,1,0:T(8,128)(2,1)S(1)}, bf16[1,64,512]{2,1,0:T(8,128)(2,1)}, u32[]{:S(2)}) copy-start(bf16[1,64,512]{2,1,0:T(8,128)(2,1)} %get-tuple-element.90) | copy-start | bytes 196612
  241.2 14.4 %copy-start.49 = (bf16[1,64,512]{2,1,0:T(8,128)(2,1)S(1)}, bf16[1,64,512]{2,1,0:T(8,128)(2,1)}, u32[]{:S(2)}) copy-start(bf16[1,64,512]{2,1,0:T(8,128)(2,1)} %get-tuple-element.89) | copy-start | bytes 196612
  241.9 14.5 %copy-start.48 = (bf16[1,64,512]{2,1,0:T(8,128)(2,1)S(1)}, bf16[1,64,512]{2,1,0:T(8,128)(2,1)}, u32[]{:S(2)}) copy-start(bf16[1,64,512]{2,1,0:T(8,128)(2,1)} %get-tuple-element.88) | copy-start | bytes 196612
  242.6 14.5 %copy-start.47 = (bf16[1,64,512]{2,1,0:T(8,128)(2,1)S(1)}, bf16[1,64,512]{2,1,0:T(8,128)(2,1)}, u32[]{:S(2)}) copy-start(bf16[1,64,512]{2,1,0:T(8,128)(2,1)} %get-tuple-element.87) | copy-start | bytes 196612
  243.3 14.5 %copy-start.46 = (bf16[1,64,512]{2,1,0:T(8,128)(2,1)S(1)}, bf16[1,64,512]{2,1,0:T(8,128)(2,1)}, u32[]{:S(2)}) copy-start(bf16[1,64,512]{2,1,0:T(8,128)(2,1)} %get-tuple-element.86) | copy-start | bytes 196612
  243.9 14.5 %copy-start.45 = (bf16[1,64,512]{2,1,0:T(8,128)(2,1)S(1)}, bf16[1,64,512]{2,1,0:T(8,128)(2,1)}, u32[]{:S(2)}) copy-start(bf16[1,64,512]{2,1,0:T(8,128)(2,1)} %get-tuple-element.85) | copy-start | bytes 196612
  244.6 14.5 %copy-start.44 = (bf16[1,64,512]{2,1,0:T(8,128)(2,1)S(1)}, bf16[1,64,512]{2,1,0:T(8,128)(2,1)}, u32[]{:S(2)}) copy-start(bf16[1,64,512]{2,1,0:T(8,128)(2,1)} %get-tuple-element.84) | copy-start | bytes 196612
  275.1 14.9 %copy-start.84 = (bf16[1,64,512]{2,1,0:T(8,128)(2,1)S(1)}, bf16[1,64,512]{2,1,0:T(8,128)(2,1)}, u32[]{:S(2)}) copy-start(bf16[1,64,512]{2,1,0:T(8,128)(2,1)} %get-tuple-element.173) | copy-start | bytes 196612
  275.1 15.6 %copy-start.81 = (bf16[1,64,512]{2,1,0:T(8,128)(2,1)S(1)}, bf16[1,64,512]{2,1,0:T(8,128)(2,1)}, u32[]{:S(2)}) copy-start(bf16[1,64,512]{2,1,0:T(8,128)(2,1)} %get-tuple-element.172) | copy-start | bytes 196612
  275.1 16.3 %copy-start.78 = (bf16[1,64,512]{2,1,0:T(8,128)(2,1)S(1)}, bf16[1,64,512]{2,1,0:T(8,128)(2,1)}, u32[]{:S(2)}) copy-start(bf16[1,64,512]{2,1,0:T(8,128)(2,1)} %get-tuple-element.171) | copy-start | bytes 196612
  275.1 16.9 %copy-start.75 = (bf16[1,64,512]{2,1,0:T(8,128)(2,1)S(1)}, bf16[1,64,512]{2,1,0:T(8,128)(2,1)}, u32[]{:S(2)}) copy-start(bf16[1,64,512]{2,1,0:T(8,128)(2,1)} %get-tuple-element.170) | copy-start | bytes 196612
  275.1 17.6 %copy-start.72 = (bf16[1,64,512]{2,1,0:T(8,128)(2,1)S(1)}, bf16[1,64,512]{2,1,0:T(8,128)(2,1)}, u32[]{:S(2)}) copy-start(bf16[1,64,512]{2,1,0:T(8,128)(2,1)} %get-tuple-element.169) | copy-start | bytes 196612
  275.1 18.3 %copy-start.69 = (bf16[1,64,512]{2,1,0:T(8,128)(2,1)S(1)}, bf16[1,64,512]{2,1,0:T(8,128)(2,1)}, u32[]{:S(2)}) copy-start(bf16[1,64,512]{2,1,0:T(8,128)(2,1)} %get-tuple-element.168) | copy-start | bytes 196612
  276.4 17.7 %copy-start.66 = (bf16[1,64,512]{2,1,0:T(8,128)(2,1)S(1)}, bf16[1,64,512]{2,1,0:T(8,128)(2,1)}, u32[]{:S(2)}) copy-start(bf16[1,64,512]{2,1,0:T(8,128)(2,1)} %get-tuple-element.167) | copy-start | bytes 196612
  276.4 18.4 %copy-start.63 = (bf16[1,64,512]{2,1,0:T(8,128)(2,1)S(1)}, bf16[1,64,512]{2,1,0:T(8,128)(2,1)}, u32[]{:S(2)}) copy-start(bf16[1,64,512]{2,1,0:T(8,128)(2,1)} %get-tuple-element.166) | copy-start | bytes 196612
  277.2 18.3 %copy-start.60 = (bf16[1,64,512]{2,1,0:T(8,128)(2,1)S(1)}, bf16[1,64,512]{2,1,0:T(8,128)(2,1)}, u32[]{:S(2)}) copy-start(bf16[1,64,512]{2,1,0:T(8,128)(2,1)} %get-tuple-element.165) | copy-start | bytes 196612
  277.2 19.0 %copy-start.58 = (bf16[1,64,512]{2,1,0:T(8,128)(2,1)S(1)}, bf16[1,64,512]{2,1,0:T(8,128)(2,1)}, u32[]{:S(2)}) copy-start(bf16[1,64,512]{2,1,0:T(8,128)(2,1)} %get-tuple-element.164) | copy-start | bytes 196612
  278.1 18.8 %copy-start.56 = (bf16[1,64,512]{2,1,0:T(8,128)(2,1)S(1)}, bf16[1,64,512]{2,1,0:T(8,128)(2,1)}, u32[]{:S(2)}) copy-start(bf16[1,64,512]{2,1,0:T(8,128)(2,1)} %get-tuple-element.163) | copy-start | bytes 196612
  279.7 17.9 %copy-start.54 = (bf16[1,64,512]{2,1,0:T(8,128)(2,1)S(1)}, bf16[1,64,512]{2,1,0:T(8,128)(2,1)}, u32[]{:S(2)}) copy-start(bf16[1,64,512]{2,1,0:T(8,128)(2,1)} %get-tuple-element.162) | copy-start | bytes 196612
  281.2 17.0 %copy-start.52 = (bf16[1,64,512]{2,1,0:T(8,128)(2,1)S(1)}, bf16[1,64,512]{2,1,0:T(8,128)(2,1)}, u32[]{:S(2)}) copy-start(bf16[1,64,512]{2,1,0:T(8,128)(2,1)} %get-tuple-element.161) | copy-start | bytes 196612
  282.8 16.2 %copy-start.50 = (bf16[1,64,512]{2,1,0:T(8,128)(2,1)S(1)}, bf16[1,64,512]{2,1,0:T(8,128)(2,1)}, u32[]{:S(2)}) copy-start(bf16[1,64,512]{2,1,0:T(8,128)(2,1)} %get-tuple-element.160) | copy-start | bytes 196612
  284.3 15.3 %copy-start.27 = (bf16[1,64,512]{2,1,0:T(8,128)(2,1)S(1)}, bf16[1,64,512]{2,1,0:T(8,128)(2,1)}, u32[]{:S(2)}) copy-start(bf16[1,64,512]{2,1,0:T(8,128)(2,1)} %get-tuple-element.121) | copy-start | bytes 196612
  285.9 14.5 %copy-start.25 = (bf16[1,64,512]{2,1,0:T(8,128)(2,1)S(1)}, bf16[1,64,512]{2,1,0:T(8,128)(2,1)}, u32[]{:S(2)}) copy-start(bf16[1,64,512]{2,1,0:T(8,128)(2,1)} %get-tuple-element.120) | copy-start | bytes 196612
  286.6 14.5 %copy-start.23 = (bf16[1,64,512]{2,1,0:T(8,128)(2,1)S(1)}, bf16[1,64,512]{2,1,0:T(8,128)(2,1)}, u32[]{:S(2)}) copy-start(bf16[1,64,512]{2,1,0:T(8,128)(2,1)} %get-tuple-element.119) | copy-start | bytes 196612
  287.3 14.5 %copy-start.21 = (bf16[1,64,512]{2,1,0:T(8,128)(2,1)S(1)}, bf16[1,64,512]{2,1,0:T(8,128)(2,1)}, u32[]{:S(2)}) copy-start(bf16[1,64,512]{2,1,0:T(8,128)(2,1)} %get-tuple-element.118) | copy-start | bytes 196612
  288.0 14.5 %copy-start.19 = (bf16[1,64,512]{2,1,0:T(8,128)(2,1)S(1)}, bf16[1,64,512]{2,1,0:T(8,128)(2,1)}, u32[]{:S(2)}) copy-start(bf16[1,64,512]{2,1,0:T(8,128)(2,1)} %get-tuple-element.117) | copy-start | bytes 196612
  288.6 14.5 %copy-start.17 = (bf16[1,64,512]{2,1,0:T(8,128)(2,1)S(1)}, bf16[1,64,512]{2,1,0:T(8,128)(2,1)}, u32[]{:S(2)}) copy-start(bf16[1,64,512]{2,1,0:T(8,128)(2,1)} %get-tuple-element.116) | copy-start | bytes 196612
  319.7 14.8 %copy-start.29 = (bf16[1,64,512]{2,1,0:T(8,128)(2,1)S(1)}, bf16[1,64,512]{2,1,0:T(8,128)(2,1)}, u32[]{:S(2)}) copy-start(bf16[1,64,512]{2,1,0:T(8,128)(2,1)} %get-tuple-element.236) | copy-start | bytes 196612
  319.7 15.4 %copy-start.28 = (bf16[1,64,512]{2,1,0:T(8,128)(2,1)S(1)}, bf16[1,64,512]{2,1,0:T(8,128)(2,1)}, u32[]{:S(2)}) copy-start(bf16[1,64,512]{2,1,0:T(8,128)(2,1)} %get-tuple-element.197) | copy-start | bytes 196612
  320.5 15.3 %copy-start.26 = (bf16[1,64,512]{2,1,0:T(8,128)(2,1)S(1)}, bf16[1,64,512]{2,1,0:T(8,128)(2,1)}, u32[]{:S(2)}) copy-start(bf16[1,64,512]{2,1,0:T(8,128)(2,1)} %get-tuple-element.196) | copy-start | bytes 196612
  320.5 16.0 %copy-start.24 = (bf16[1,64,512]{2,1,0:T(8,128)(2,1)S(1)}, bf16[1,64,512]{2,1,0:T(8,128)(2,1)}, u32[]{:S(2)}) copy-start(bf16[1,64,512]{2,1,0:T(8,128)(2,1)} %get-tuple-element.195) | copy-start | bytes 196612
  320.5 16.7 %copy-start.22 = (bf16[1,64,512]{2,1,0:T(8,128)(2,1)S(1)}, bf16[1,64,512]{2,1,0:T(8,128)(2,1)}, u32[]{:S(2)}) copy-start(bf16[1,64,512]{2,1,0:T(8,128)(2,1)} %get-tuple-element.194) | copy-start | bytes 196612
  320.6 17.3 %copy-start.20 = (bf16[1,64,512]{2,1,0:T(8,128)(2,1)S(1)}, bf16[1,64,512]{2,1,0:T(8,128)(2,1)}, u32[]{:S(2)}) copy-start(bf16[1,64,512]{2,1,0:T(8,128)(2,1)} %get-tuple-element.193) | copy-start | bytes 196612
  321.5 17.1 %copy-start.18 = (bf16[1,64,512]{2,1,0:T(8,128)(2,1)S(1)}, bf16[1,64,512]{2,1,0:T(8,128)(2,1)}, u32[]{:S(2)}) copy-start(bf16[1,64,512]{2,1,0:T(8,128)(2,1)} %get-tuple-element.192) | copy-start | bytes 196612
  323.1 16.2 %copy-start.16 = (bf16[1,64,512]{2,1,0:T(8,128)(2,1)S(1)}, bf16[1,64,512]{2,1,0:T(8,128)(2,1)}, u32[]{:S(2)}) copy-start(bf16[1,64,512]{2,1,0:T(8,128)(2,1)} %get-tuple-element.191) | copy-start | bytes 196612
  324.6 15.3 %copy-start.15 = (bf16[1,64,512]{2,1,0:T(8,128)(2,1)S(1)}, bf16[1,64,512]{2,1,0:T(8,128)(2,1)}, u32[]{:S(2)}) copy-start(bf16[1,64,512]{2,1,0:T(8,128)(2,1)} %get-tuple-element.190) | copy-start | bytes 196612
  326.1 14.5 %copy-start.14 = (bf16[1,64,512]{2,1,0:T(8,128)(2,1)S(1)}, bf16[1,64,512]{2,1,0:T(8,128)(2,1)}, u32[]{:S(2)}) copy-start(bf16[1,64,512]{2,1,0:T(8,128)(2,1)} %get-tuple-element.189) | copy-start | bytes 196612
  326.8 14.5 %copy-start.13 = (bf16[1,64,512]{2,1,0:T(8,128)(2,1)S(1)}, bf16[1,64,512]{2,1,0:T(8,128)(2,1)}, u32[]{:S(2)}) copy-start(bf16[1,64,512]{2,1,0:T(8,128)(2,1)} %get-tuple-element.188) | copy-start | bytes 196612
  327.5 14.5 %copy-start.12 = (bf16[1,64,512]{2,1,0:T(8,128)(2,1)S(1)}, bf16[1,64,512]{2,1,0:T(8,128)(2,1)}, u32[]{:S(2)}) copy-start(bf16[1,64,512]{2,1,0:T(8,128)(2,1)} %get-tuple-element.187) | copy-start | bytes 196612
  328.2 14.5 %copy-start.11 = (bf16[1,64,512]{2,1,0:T(8,128)(2,1)S(1)}, bf16[1,64,512]{2,1,0:T(8,128)(2,1)}, u32[]{:S(2)}) copy-start(bf16[1,64,512]{2,1,0:T(8,128)(2,1)} %get-tuple-element.186) | copy-start | bytes 196612
  328.9 14.4 %copy-start.102 = (bf16[1,64,512]{2,1,0:T(8,128)(2,1)S(1)}, bf16[1,64,512]{2,1,0:T(8,128)(2,1)}, u32[]{:S(2)}) copy-start(bf16[1,64,512]{2,1,0:T(8,128)(2,1)} %get-tuple-element.255) | copy-start | bytes 196612
  379.0 15.5 %copy-start.148 = (bf16[64,1,4,128]{3,2,0,1:T(4,128)(2,1)S(1)}, bf16[64,1,4,128]{3,2,0,1:T(4,128)(2,1)}, u32[]{:S(2)}) copy-start(bf16[64,1,4,128]{3,2,0,1:T(4,128)(2,1)} %stack.875) | copy-start | bytes 196612
  379.0 14.8 %copy-start.149 = (bf16[64,1,4,128]{3,2,0,1:T(4,128)(2,1)S(1)}, bf16[64,1,4,128]{3,2,0,1:T(4,128)(2,1)}, u32[]{:S(2)}) copy-start(bf16[64,1,4,128]{3,2,0,1:T(4,128)(2,1)} %stack.874) | copy-start | bytes 196612
  434.6 13.7 %collective-permute-start.1 = (bf16[2,256,512]{2,1,0:T(8,128)(2,1)}, bf16[2,256,512]{2,1,0:T(8,128)(2,1)S(1)}, u32[]{:S(2)}, u32[]{:S(2)}) collective-permute-start(bf16[2,256,512]{2,1,0:T(8,128)(2,1)} %collective-permute-done), channel_id=1, source_target_pairs={{0,2},{2,4},{4,6},{6,8},{8,10},{10,12},{12,14},{14,16},{16,18},{18... | collective-permute-start | bytes 1572872 | tf_op jit(solution)/shard_map/ppermute | solution.py:17
  601.9 28.6 %copy-start.9 = (bf16[576,4,128]{2,1,0:T(4,128)(2,1)S(1)}, bf16[576,4,128]{2,1,0:T(4,128)(2,1)}, u32[]{:S(2)}) copy-start(bf16[576,4,128]{2,1,0:T(4,128)(2,1)} %slice.1480) | copy-start | bytes 1769476
  704.2 206.8 %all-gather.5.cloned.1.call-start = ((), (), s32[]{:S(2)}) async-start(), calls=%async_computation.1 | async-start | bytes 17825792 | tf_op jit(solution)/shard_map/all_gather | solution.py:112
  (110 other events, 1103.8 us)
Sparse Core Ops, SparseCore 0:
  704.3 11.0 all-gather.2
  718.2 192.7 all-gather.4
where the time goes:
time: 949 us; the launch traced here: 930 us
  local copies, waits for them, and re-layouts  410 us (43%)
  waiting for transfers between devices  213 us (22%)
  other arithmetic  145 us (15%)
  matrix products  134 us (14%)
  between operations  16.6 us (2%)
  starting transfers between devices  12.1 us (1%)
    all_gather x1, waiting for transfers between devices, on_device(): lax.all_gather(out_weight, 'seq', axis=0, tiled=True)  196 us
    another operation x132, local copies, waits for them, and re-layouts, on_device(): jnp.stack([near_v[SECOND_WINDOW - 1 - lag_step:SECOND_WINDOW - 1 - lag_st...  155 us
    another operation x132, local copies, waits for them, and re-layouts, on_device(): jnp.stack([near_k[SECOND_WINDOW - 1 - lag_step:SECOND_WINDOW - 1 - lag_st...  133 us
    reduce_sum x4, other arithmetic, attend_block(): row_sum = jnp.sum(row_weights, axis=(3, 4))  114 us
    dot_general x4, matrix products, attend_block(): jnp.einsum('itvgd,jvd->ivgtj', query_mod, first_rows, preferred_element_t...  76.7 us
    unnamed x465, local copies, waits for them, and re-layouts  73.3 us
    dot_general x4, matrix products, attend_block(): jnp.einsum('ivgtj,jvd->ivgtd', weights_bf, first_vals, preferred_element_...  45.7 us
  transfers between devices with their start and end apart: 5, of which 3 were waited for; matrix products, arithmetic and copies ran while one was open for 45% of the time, Pallas kernels for 0%

commit v1 on v0

v1 whole, which is shorter than its diff:
```python
import math

import jax
import jax.numpy as jnp
from jax import lax
from jax.experimental import pallas as pl
from jax.experimental.pallas import tpu as pltpu
from jax.sharding import PartitionSpec as P

HEAD_SIZE = 128
GROUP_QUERIES = 2
FIRST_WINDOW = 512
SECOND_WINDOW = 32
SUB = 32
OFFSETS = 8
NEG = -1e30
EXP2_SCALE = HEAD_SIZE ** (-0.5) * math.log2(math.e)


def passed_along(x, axis, by):
    size = lax.axis_size(axis)
    pairs = [(i, i + by) for i in range(size) if 0 <= i + by < size]
    return lax.ppermute(x, axis, pairs)


def attend_kernel(first_ref, q_ref, k_ref, v_ref, k2_ref, v2_ref, out_ref, s_ref, m_ref):
    b = pl.program_id(1)
    base = pl.multiple_of(b * SUB, SUB)
    query_first = first_ref[0] + base
    rows_t = GROUP_QUERIES * SUB
    rows = OFFSETS * rows_t
    q = [
        q_ref[:, g * HEAD_SIZE : (g + 1) * HEAD_SIZE].astype(jnp.float32)
        for g in range(GROUP_QUERIES)
    ]
    key_pos = query_first - FIRST_WINDOW + lax.broadcasted_iota(jnp.int32, (1, FIRST_WINDOW), 1)
    bias = jnp.where(key_pos >= 0, 0.0, NEG).astype(jnp.float32)
    lane = lax.broadcasted_iota(jnp.int32, (rows, 128), 1)
    token = lax.rem(lax.broadcasted_iota(jnp.int32, (rows, 128), 0), SUB)
    is_new = lane <= token
    contract = (((1,), (1,)), ((), ()))

    def near(ref, t):
        return ref[pl.ds(base + SECOND_WINDOW - t, SUB), :]

    def fold(s, top):
        s4 = s.reshape(OFFSETS, rows_t, FIRST_WINDOW)
        for tt in range(OFFSETS):
            for c in range(FIRST_WINDOW // 128):
                top = jnp.maximum(top, s4[tt, :, c * 128 : (c + 1) * 128])
        return top

    def scores_step(c, top):
        parts = []
        for tt in range(OFFSETS):
            k2 = near(k2_ref, c * OFFSETS + tt)
            for g in range(GROUP_QUERIES):
                parts.append((q[g] * k2).astype(jnp.bfloat16))
        query_mod = jnp.concatenate(parts, axis=0)
        old = lax.dot_general(
            query_mod,
            k_ref[pl.ds(base, FIRST_WINDOW), :],
            contract,
            preferred_element_type=jnp.float32,
        )
        old = old + bias
        new = lax.dot_general(
            query_mod,
            k_ref[pl.ds(base + FIRST_WINDOW, 128), :],
            contract,
            preferred_element_type=jnp.float32,
        )
        s = jnp.concatenate([jnp.where(is_new, new, old[:, :128]), old[:, 128:]], axis=1)
        s_ref[pl.ds(pl.multiple_of(c * rows, rows), rows), :] = s
        return fold(s, top)

    steps = SECOND_WINDOW // OFFSETS
    low = jnp.full((rows_t, 128), NEG, jnp.float32)
    m_ref[...] = lax.fori_loop(0, steps, scores_step, low)

    @pl.when(query_first < SECOND_WINDOW)
    def _():
        def mask_step(c, top):
            at = pl.ds(pl.multiple_of(c * rows, rows), rows)
            row = lax.broadcasted_iota(jnp.int32, (rows, FIRST_WINDOW), 0)
            offset = c * OFFSETS + row // rows_t
            ok = query_first + lax.rem(row, SUB) - offset >= 0
            s = jnp.where(ok, s_ref[at, :], NEG)
            s_ref[at, :] = s
            return fold(s, top)

        m_ref[...] = lax.fori_loop(0, steps, mask_step, low)

    shift = jnp.max(m_ref[...], axis=1, keepdims=True) * EXP2_SCALE
    shift = jnp.broadcast_to(shift, (rows_t, 128))
    shift_all = jnp.concatenate([shift] * (FIRST_WINDOW // 128), axis=1)
    ones = jnp.ones((FIRST_WINDOW, HEAD_SIZE), jnp.bfloat16)

    def mix_step(c, carry):
        total, weight = carry
        s = s_ref[pl.ds(pl.multiple_of(c * rows, rows), rows), :]
        s = s.reshape(OFFSETS, rows_t, FIRST_WINDOW) * EXP2_SCALE - shift_all[None]
        p = jnp.exp2(s).reshape(rows, FIRST_WINDOW)
        p_old = jnp.concatenate(
            [jnp.where(is_new, 0.0, p[:, :128]).astype(jnp.bfloat16), p[:, 128:].astype(jnp.bfloat16)],
            axis=1,
        )
        p_new = jnp.where(is_new, p[:, :128], 0.0).astype(jnp.bfloat16)
        v_old = jnp.concatenate([v_ref[pl.ds(base, FIRST_WINDOW), :], ones], axis=1)
        v_new = jnp.concatenate([v_ref[pl.ds(base + FIRST_WINDOW, 128), :], ones[:128]], axis=1)
        mix = jnp.dot(p_old, v_old, preferred_element_type=jnp.float32) + jnp.dot(
            p_new, v_new, preferred_element_type=jnp.float32
        )
        for tt in range(OFFSETS):
            v2 = near(v2_ref, c * OFFSETS + tt)
            v2 = jnp.concatenate([v2] * GROUP_QUERIES, axis=0)
            part = mix[tt * rows_t : (tt + 1) * rows_t]
            total = total + part[:, :HEAD_SIZE] * v2
            weight = weight + part[:, HEAD_SIZE:]
        return total, weight

    zero = jnp.zeros((rows_t, HEAD_SIZE), jnp.float32)
    total, weight = lax.fori_loop(0, steps, mix_step, (zero, zero))
    result = (total / weight).astype(jnp.bfloat16)
    for g in range(GROUP_QUERIES):
        out_ref[:, g * HEAD_SIZE : (g + 1) * HEAD_SIZE] = result[g * SUB : (g + 1) * SUB]


def attend(first, queries, keys, values, near_keys, near_values):
    local_rows = queries.shape[0]
    kv_local = keys.shape[1] // HEAD_SIZE
    width = GROUP_QUERIES * HEAD_SIZE
    rows = local_rows * kv_local * GROUP_QUERIES * SECOND_WINDOW

    def whole(x):
        return pl.BlockSpec((x.shape[0], HEAD_SIZE), lambda v, b, first: (0, v))

    block = pl.BlockSpec((SUB, width), lambda v, b, first: (b, v))
    return pl.pallas_call(
        attend_kernel,
        out_shape=jax.ShapeDtypeStruct(queries.shape, jnp.bfloat16),
        grid_spec=pltpu.PrefetchScalarGridSpec(
            num_scalar_prefetch=1,
            grid=(kv_local, local_rows // SUB),
            in_specs=[block, whole(keys), whole(values), whole(near_keys), whole(near_values)],
            out_specs=block,
            scratch_shapes=[
                pltpu.VMEM((SECOND_WINDOW * GROUP_QUERIES * SUB, FIRST_WINDOW), jnp.float32),
                pltpu.VMEM((GROUP_QUERIES * SUB, 128), jnp.float32),
            ],
        ),
        compiler_params=pltpu.CompilerParams(vmem_limit_bytes=40 * 1024 * 1024),
        cost_estimate=pl.CostEstimate(
            flops=rows * 2 * 2 * 768 * 256, bytes_accessed=8 << 20, transcendentals=rows * 512
        ),
    )(first, queries, keys, values, near_keys, near_values)


def on_device(
    queries, first_pair_keys, first_pair_values, second_pair_keys, second_pair_values, out_weight
):
    local_rows, columns = queries.shape
    width = first_pair_keys.shape[1]
    seq_index = lax.axis_index("seq")
    hop_count = FIRST_WINDOW // local_rows
    all_weight = lax.all_gather(out_weight, "seq", axis=0, tiled=True)
    pair = jnp.concatenate([first_pair_keys, first_pair_values], axis=1)
    near = jnp.concatenate([second_pair_keys, second_pair_values], axis=1)
    parts = [passed_along(pair, "seq", hop) for hop in range(hop_count, 0, -1)] + [
        pair,
        jnp.zeros((128, 2 * width), jnp.bfloat16),
    ]
    window = jnp.concatenate(parts, axis=0)
    edge = passed_along(near[local_rows - SECOND_WINDOW :], "seq", 1)
    near = jnp.concatenate([edge, near], axis=0).astype(jnp.float32)
    attended = attend(
        (seq_index * local_rows).astype(jnp.int32)[None],
        queries,
        window[:, :width],
        window[:, width:],
        near[:, :width],
        near[:, width:],
    )
    heads = lax.axis_size("head")
    me = lax.axis_index("head")
    all_heads = jnp.zeros((local_rows, heads * columns), jnp.bfloat16)
    all_heads = lax.dynamic_update_slice(all_heads, attended, (0, me * columns))
    for k in range(1, heads):
        other = lax.ppermute(attended, "head", [(i, (i + k) % heads) for i in range(heads)])
        at = lax.rem(me + heads - k, heads) * columns
        all_heads = lax.dynamic_update_slice(all_heads, other, (0, at))
    projected = jnp.dot(all_heads, all_weight, preferred_element_type=jnp.float32)
    return (attended, projected.astype(jnp.bfloat16))


def solution(mesh):
    spec = P("seq", "head")
    return jax.shard_map(
        on_device, mesh=mesh, in_specs=(spec,) * 6, out_specs=(spec, spec), check_vma=False
    )
```

time: 949 us -> 237 us (0.25); the launches traced: 930 us -> 237 us
  local copies, waits for them, and re-layouts: 410 us -> 4.39 us
  other arithmetic: 145 us -> 0.46 us
  matrix products: 134 us -> 11.4 us
  waiting for transfers between devices: 213 us -> 93.9 us
  Pallas kernels: 0 us -> 100 us
    another operation x265 -> x0, local copies, waits for them, and re-layouts: 289 us -> none  [the longest x132 155 us: on_device(): jnp.stack([near_v[SECOND_WINDOW - 1 - lag_step:SECOND_WINDOW - 1 - lag_st...]
    all_gather x2 -> x1, waiting for transfers between devices: 206 us -> 68.2 us  [on_device(): all_weight = lax.all_gather(out_weight, 'seq', axis=0, tiled=True)]
    dot_general x9 -> x1, matrix products: 134 us -> 11.4 us  [on_device(): jnp.dot(all_heads, all_weight, preferred_element_type=jnp.float32)]
    reduce_sum x4 -> x0, other arithmetic: 114 us -> none  [attend_block(): row_sum = jnp.sum(row_weights, axis=(3, 4))]
    pallas_call x0 -> x1, Pallas kernels: none -> 100 us  [attend(): pl.pallas_call(attend_kernel, out_shape=jax.ShapeDtypeStruct(queries.shap...]
    unnamed x465 -> x8, local copies, waits for them, and re-layouts: 73.3 us -> 1.9 us
    slice x25 -> x3, local copies, waits for them, and re-layouts: 28.6 us -> 0.24 us  [the longest x1 0.14 us: on_device(): window[:, width:]]
    convert_element_type x20 -> x0, local copies, waits for them, and re-layouts: 18.9 us -> none  [the longest x4 13.1 us: attend_block(): second_win.astype(jnp.float32)[:, :, :, None, :]]
  transfers between devices with their start and end apart: 5 -> 5, of which waited for: 3 -> 4; matrix products, arithmetic and copies ran while one was open for 45% -> 2% of each run, Pallas kernels for 0% -> 42%
where the time goes in v1:
time: 237 us
  Pallas kernels  100 us (42%)
  waiting for transfers between devices  93.9 us (40%)
  between operations  14.2 us (6%)
  starting transfers between devices  11.7 us (5%)
  matrix products  11.4 us (5%)
  local copies, waits for them, and re-layouts  4.39 us (2%)
    pallas_call x1, Pallas kernels, attend(): pl.pallas_call(attend_kernel, out_shape=jax.ShapeDtypeStruct(queries.shap...  100 us
    all_gather x1, waiting for transfers between devices, on_device(): all_weight = lax.all_gather(out_weight, 'seq', axis=0, tiled=True)  68.2 us
    ppermute x3, waiting for transfers between devices, passed_along(): return lax.ppermute(x, axis, pairs)  24.1 us
    ppermute x3, starting transfers between devices, passed_along(): return lax.ppermute(x, axis, pairs)  11.7 us
    dot_general x1, matrix products, on_device(): jnp.dot(all_heads, all_weight, preferred_element_type=jnp.float32)  11.4 us
  transfers between devices with their start and end apart: 5, of which 4 were waited for; matrix products, arithmetic and copies ran while one was open for 2% of the time, Pallas kernels for 42%

profile of v1, /device:TPU:0, one launch (start us, length us, event | category | flops | bytes accessed | tf_op | source)
XLA Modules:
  0.0 236.6 jit_solution(916110290464500780)
XLA Ops:
  7.2 0.0 copy-start.1
  7.2 0.0 copy-start.2
  7.2 0.0 all-gather.2.cloned.1.call-start
  7.2 0.7 all-gather.2.cloned.1.call-update
  7.9 1.0 constant_dynamic-update-slice_fusion.1
  8.9 1.0 constant_dynamic-update-slice_fusion
  9.9 4.9 %collective-permute-start = (bf16[256,1024]{1,0:T(8,128)(2,1)S(1)}, bf16[256,1024]{1,0:T(8,128)(2,1)S(1)}, u32[]{:S(2)}, u32[]{:S(2)}) collective-permute-start(bf16[256,1024]{1,0:T(8,128)(2,1)S(1)} %constant_dynamic-update-slice_fusion), channel_id=1, source_target_pairs={{0,4},{2,6},{4,8},{6,10},{8,12},{10,14},{12,16},{14,18},{16,20},{1... | collective-permute-start | bytes 1572872 | tf_op jit(solution)/shard_map/ppermute | solution.py:23
  14.8 3.4 %collective-permute-start.1 = (bf16[256,1024]{1,0:T(8,128)(2,1)S(1)}, bf16[256,1024]{1,0:T(8,128)(2,1)S(1)}, u32[]{:S(2)}, u32[]{:S(2)}) collective-permute-start(bf16[256,1024]{1,0:T(8,128)(2,1)S(1)} %constant_dynamic-update-slice_fusion), channel_id=1, source_target_pairs={{0,2},{2,4},{4,6},{6,8},{8,10},{10,12},{12,14},{14,16},{16,18},{18... | collective-permute-start | bytes 1572872 | tf_op jit(solution)/shard_map/ppermute | solution.py:23
  18.2 0.0 copy-done.1
  18.3 0.0 copy-done.2
  18.3 3.3 %collective-permute-start.2 = (bf16[32,1024]{1,0:T(8,128)(2,1)S(1)}, bf16[32,1024]{1,0:T(8,128)(2,1)S(1)}, u32[]{:S(2)}, u32[]{:S(2)}) collective-permute-start(bf16[32,1024]{1,0:T(8,128)(2,1)S(1)} %slice.22), channel_id=1, source_target_pairs={{0,2},{2,4},{4,6},{6,8},{8,10},{10,12},{12,14},{14,16},{16,18},{18... | collective-permute-start | bytes 196616 | tf_op jit(solution)/shard_map/ppermute | solution.py:23
  21.7 16.3 %collective-permute-done.2 = bf16[32,1024]{1,0:T(8,128)(2,1)S(1)} collective-permute-done((bf16[32,1024]{1,0:T(8,128)(2,1)S(1)}, bf16[32,1024]{1,0:T(8,128)(2,1)S(1)}, u32[]{:S(2)}, u32[]{:S(2)}) %collective-permute-start.2) | collective-permute-done | bytes 65568 | tf_op jit(solution)/shard_map/ppermute | solution.py:23
  38.0 0.1 maximum_convert_fusion
  38.1 0.1 fusion.1
  38.2 7.8 %collective-permute-done = bf16[256,1024]{1,0:T(8,128)(2,1)S(1)} collective-permute-done((bf16[256,1024]{1,0:T(8,128)(2,1)S(1)}, bf16[256,1024]{1,0:T(8,128)(2,1)S(1)}, u32[]{:S(2)}, u32[]{:S(2)}) %collective-permute-start) | collective-permute-done | bytes 524320 | tf_op jit(solution)/shard_map/ppermute | solution.py:23
  46.1 0.0 collective-permute-done.1
  46.1 0.3 maximum_maximum_fusion
  46.4 0.0 copy-start
  46.4 0.1 fusion
  46.6 0.9 copy-done
  47.4 100.5 %shard_map.77 = bf16[256,1024]{1,0:T(8,128)(2,1)} custom-call(s32[1]{0:T(128)} %bitcast.first_ref, bf16[256,1024]{1,0:T(8,128)(2,1)S(1)} %copy-done, bf16[896,512]{1,0:T(8,128)(2,1)S(1)} %get-tuple-element.3.k_ref, bf16[896,512]{1,0:T(8,128)(2,1)S(1)} %get-tuple-element.2.v_ref, f32[288,512]{1,0:T(8,128)S(1)} %get-tuple-element.5.k2_ref, ...), custom_call_target="tpu_custom_call" | custom-call | flops 51539607552 | bytes 8388608 | tf_op jit(solution)/shard_map/pallas_call | solution.py:139
  147.9 0.0 collective-permute-start.3
  147.9 0.1 broadcast_in_dim.11
  148.0 1.1 constant_dynamic-update-slice_fusion.5
  149.1 0.9 collective-permute-done.3
  150.1 68.2 %all-gather.2.cloned.1.call-done = bf16[2048,4096]{1,0:T(8,128)(2,1)} async-done(((bf16[128,4096]{1,0:T(8,128)(2,1)}), bf16[2048,4096]{1,0:T(8,128)(2,1)}) %all-gather.2.cloned.1.call-update) | async-done | bytes 16777232 | tf_op jit(solution)/shard_map/all_gather | solution.py:166
  218.3 11.4 %convolution_convert_fusion = bf16[256,4096]{1,0:T(8,128)(2,1)} fusion(bf16[256,2048]{1,0:T(8,128)(2,1)S(1)} %constant_dynamic-update-slice_fusion.4, bf16[2048,4096]{1,0:T(8,128)(2,1)} %all-gather.2.cloned.1.call-done), kind=kOutput, calls=%fused_computation | convolution fusion | flops 4296015872 | bytes 19922944 | tf_op jit(solution)/shard_map/dot_general | solution.py:192
  (6 shorter events, 0.1 us)
Async XLA Ops:
  7.2 11.1 %copy-start.1 = (bf16[256,512]{1,0:T(8,128)(2,1)S(1)}, bf16[256,512]{1,0:T(8,128)(2,1)}, u32[]{:S(2)}) copy-start(bf16[256,512]{1,0:T(8,128)(2,1)} %param.9) | copy-start | bytes 786436
  7.2 11.1 %copy-start.2 = (bf16[256,512]{1,0:T(8,128)(2,1)S(1)}, bf16[256,512]{1,0:T(8,128)(2,1)}, u32[]{:S(2)}) copy-start(bf16[256,512]{1,0:T(8,128)(2,1)} %param.10) | copy-start | bytes 786436
  7.2 211.1 %all-gather.2.cloned.1.call-start = ((), (), s32[]{:S(2)}) async-start(), calls=%async_computation | async-start | bytes 17825792 | tf_op jit(solution)/shard_map/all_gather | solution.py:166
  9.9 36.2 %collective-permute-start = (bf16[256,1024]{1,0:T(8,128)(2,1)S(1)}, bf16[256,1024]{1,0:T(8,128)(2,1)S(1)}, u32[]{:S(2)}, u32[]{:S(2)}) collective-permute-start(bf16[256,1024]{1,0:T(8,128)(2,1)S(1)} %constant_dynamic-update-slice_fusion), channel_id=1, source_target_pairs={{0,4},{2,6},{4,8},{6,10},{8,12},{10,14},{12,16},{14,18},{16,20},{1... | collective-permute-start | bytes 1572872 | tf_op jit(solution)/shard_map/ppermute | solution.py:23
  14.8 31.3 %collective-permute-start.1 = (bf16[256,1024]{1,0:T(8,128)(2,1)S(1)}, bf16[256,1024]{1,0:T(8,128)(2,1)S(1)}, u32[]{:S(2)}, u32[]{:S(2)}) collective-permute-start(bf16[256,1024]{1,0:T(8,128)(2,1)S(1)} %constant_dynamic-update-slice_fusion), channel_id=1, source_target_pairs={{0,2},{2,4},{4,6},{6,8},{8,10},{10,12},{12,14},{14,16},{16,18},{18... | collective-permute-start | bytes 1572872 | tf_op jit(solution)/shard_map/ppermute | solution.py:23
  18.3 19.7 %collective-permute-start.2 = (bf16[32,1024]{1,0:T(8,128)(2,1)S(1)}, bf16[32,1024]{1,0:T(8,128)(2,1)S(1)}, u32[]{:S(2)}, u32[]{:S(2)}) collective-permute-start(bf16[32,1024]{1,0:T(8,128)(2,1)S(1)} %slice.22), channel_id=1, source_target_pairs={{0,2},{2,4},{4,6},{6,8},{8,10},{10,12},{12,14},{14,16},{16,18},{18... | collective-permute-start | bytes 196616 | tf_op jit(solution)/shard_map/ppermute | solution.py:23
  46.4 1.0 copy-start
  147.9 2.1 collective-permute-start.3
Sparse Core Ops, SparseCore 0:
  10.8 207.4 all-gather.1

commit v2 on v1

--- a/solution.py
+++ b/solution.py
@@ -13,6 +13,7 @@
 SECOND_WINDOW = 32
 SUB = 32
 OFFSETS = 8
+SHARERS = 4
 NEG = -1e30
 EXP2_SCALE = HEAD_SIZE ** (-0.5) * math.log2(math.e)
 
@@ -126,24 +127,24 @@
         out_ref[:, g * HEAD_SIZE : (g + 1) * HEAD_SIZE] = result[g * SUB : (g + 1) * SUB]
 
 
-def attend(first, queries, keys, values, near_keys, near_values):
+def attend(first, split, splits, queries, keys, values, near_keys, near_values):
     local_rows = queries.shape[0]
-    kv_local = keys.shape[1] // HEAD_SIZE
+    kv_part = keys.shape[1] // HEAD_SIZE // splits
     width = GROUP_QUERIES * HEAD_SIZE
-    rows = local_rows * kv_local * GROUP_QUERIES * SECOND_WINDOW
+    rows = local_rows * kv_part * GROUP_QUERIES * SECOND_WINDOW
 
     def whole(x):
-        return pl.BlockSpec((x.shape[0], HEAD_SIZE), lambda v, b, first: (0, v))
-
-    block = pl.BlockSpec((SUB, width), lambda v, b, first: (b, v))
+        return pl.BlockSpec((x.shape[0], HEAD_SIZE), lambda v, b, first: (0, split * kv_part + v))
+
     return pl.pallas_call(
         attend_kernel,
-        out_shape=jax.ShapeDtypeStruct(queries.shape, jnp.bfloat16),
+        out_shape=jax.ShapeDtypeStruct((local_rows, kv_part * width), jnp.bfloat16),
         grid_spec=pltpu.PrefetchScalarGridSpec(
             num_scalar_prefetch=1,
-            grid=(kv_local, local_rows // SUB),
-            in_specs=[block, whole(keys), whole(values), whole(near_keys), whole(near_values)],
-            out_specs=block,
+            grid=(kv_part, local_rows // SUB),
+            in_specs=[pl.BlockSpec((SUB, width), lambda v, b, first: (b, split * kv_part + v))]
+            + [whole(x) for x in (keys, values, near_keys, near_values)],
+            out_specs=pl.BlockSpec((SUB, width), lambda v, b, first: (b, v)),
             scratch_shapes=[
                 pltpu.VMEM((SECOND_WINDOW * GROUP_QUERIES * SUB, FIRST_WINDOW), jnp.float32),
                 pltpu.VMEM((GROUP_QUERIES * SUB, 128), jnp.float32),
@@ -156,16 +157,38 @@
     )(first, queries, keys, values, near_keys, near_values)
 
 
+def within_group(x, group, by):
+    size = lax.axis_size("seq")
+    pairs = [(i, i // group * group + (i + by) % group) for i in range(size)]
+    return lax.ppermute(x, "seq", pairs)
+
+
 def on_device(
     queries, first_pair_keys, first_pair_values, second_pair_keys, second_pair_values, out_weight
 ):
     local_rows, columns = queries.shape
     width = first_pair_keys.shape[1]
+    weight_rows, features = out_weight.shape
+    seq_size = lax.axis_size("seq")
     seq_index = lax.axis_index("seq")
-    hop_count = FIRST_WINDOW // local_rows
-    all_weight = lax.all_gather(out_weight, "seq", axis=0, tiled=True)
+    heads = lax.axis_size("head")
+    me = lax.axis_index("head")
+    group = math.gcd(SHARERS, seq_size)
+    member = lax.rem(seq_index, group)
+    part = features // group
+
     pair = jnp.concatenate([first_pair_keys, first_pair_values], axis=1)
     near = jnp.concatenate([second_pair_keys, second_pair_values], axis=1)
+
+    share = jnp.zeros((group * weight_rows, part), jnp.bfloat16)
+    for k in range(group):
+        to = lax.rem(member + k, group)
+        piece = lax.dynamic_slice(out_weight, (0, to * part), (weight_rows, part))
+        if k:
+            piece = within_group(piece, group, k)
+        source = lax.rem(member + group - k, group)
+        share = lax.dynamic_update_slice(share, piece, (source * weight_rows, 0))
+    hop_count = FIRST_WINDOW // local_rows
     parts = [passed_along(pair, "seq", hop) for hop in range(hop_count, 0, -1)] + [
         pair,
         jnp.zeros((128, 2 * width), jnp.bfloat16),
@@ -173,24 +196,55 @@
     window = jnp.concatenate(parts, axis=0)
     edge = passed_along(near[local_rows - SECOND_WINDOW :], "seq", 1)
     near = jnp.concatenate([edge, near], axis=0).astype(jnp.float32)
-    attended = attend(
-        (seq_index * local_rows).astype(jnp.int32)[None],
-        queries,
-        window[:, :width],
-        window[:, width:],
-        near[:, :width],
-        near[:, width:],
+    share, queries = lax.optimization_barrier((share, queries))
+    my_weight = lax.all_gather(
+        share,
+        "seq",
+        axis=0,
+        tiled=True,
+        axis_index_groups=[list(range(p, seq_size, group)) for p in range(group)],
     )
-    heads = lax.axis_size("head")
-    me = lax.axis_index("head")
-    all_heads = jnp.zeros((local_rows, heads * columns), jnp.bfloat16)
-    all_heads = lax.dynamic_update_slice(all_heads, attended, (0, me * columns))
-    for k in range(1, heads):
-        other = lax.ppermute(attended, "head", [(i, (i + k) % heads) for i in range(heads)])
-        at = lax.rem(me + heads - k, heads) * columns
-        all_heads = lax.dynamic_update_slice(all_heads, other, (0, at))
-    projected = jnp.dot(all_heads, all_weight, preferred_element_type=jnp.float32)
-    return (attended, projected.astype(jnp.bfloat16))
+
+    splits = math.gcd(2, width // HEAD_SIZE)
+    split_columns = columns // splits
+    all_heads = jnp.zeros((group * local_rows, heads * columns), jnp.bfloat16)
+    attended = []
+    for split in range(splits):
+        mine = attend(
+            (seq_index * local_rows).astype(jnp.int32)[None],
+            split,
+            splits,
+            queries,
+            window[:, :width],
+            window[:, width:],
+            near[:, :width],
+            near[:, width:],
+        )
+        attended.append(mine)
+        tokens = jnp.concatenate(
+            [mine] + [within_group(mine, group, k) for k in range(1, group)], axis=0
+        )
+        for k in range(heads):
+            other = tokens
+            if k:
+                other = lax.ppermute(tokens, "head", [(i, (i + k) % heads) for i in range(heads)])
+            at = lax.rem(me + heads - k, heads) * columns + split * split_columns
+            all_heads = lax.dynamic_update_slice(all_heads, other, (0, at))
+    attended = jnp.concatenate(attended, axis=1)
+
+    projected = jnp.zeros((local_rows, features), jnp.bfloat16)
+    for k in list(range(1, group)) + [0]:
+        block = jnp.dot(
+            all_heads[k * local_rows : (k + 1) * local_rows],
+            my_weight,
+            preferred_element_type=jnp.float32,
+        ).astype(jnp.bfloat16)
+        if k:
+            block = within_group(block, group, group - k)
+        projected = lax.dynamic_update_slice(
+            projected, block, (0, lax.rem(member + k, group) * part)
+        )
+    return (attended, projected)
 
 
 def solution(mesh):

time: 237 us -> 235 us (level)
  waiting for transfers between devices: 93.9 us -> 53.3 us
  starting transfers between devices: 11.7 us -> 34.5 us
  local copies, waits for them, and re-layouts: 4.39 us -> 16 us
  other arithmetic: 0.46 us -> 5.93 us
    all_gather x1, waiting for transfers between devices: 68.2 us -> 0.01 us  [on_device(): lax.all_gather(share, 'seq', axis=0, tiled=True, axis_index_groups=[list(...]
    ppermute x1 -> x14, waiting for transfers between devices: 0.91 us -> 50.2 us  [the longest x12 47.6 us: within_group(): return lax.ppermute(x, 'seq', pairs)]
    ppermute x1 -> x14, starting transfers between devices: 0.01 us -> 22.8 us  [the longest x12 22.8 us: within_group(): return lax.ppermute(x, 'seq', pairs)]
    ppermute x3, waiting for transfers between devices: 24.1 us -> 3.08 us  [passed_along(): return lax.ppermute(x, axis, pairs)]
    concatenate x0 -> x3, other arithmetic: none -> 4.38 us  [the longest x2 3.52 us: on_device(): jnp.concatenate([mine] + [within_group(mine, group, k) for k in range(1,...]
    unnamed x8 -> x16, local copies, waits for them, and re-layouts: 1.9 us -> 6.26 us
    dynamic_update_slice x1 -> x2, local copies, waits for them, and re-layouts: 0.05 us -> 3.43 us  [on_device(): all_heads = lax.dynamic_update_slice(all_heads, other, (0, at))]
    dot_general x1 -> x4, matrix products: 11.4 us -> 10 us  [on_device(): jnp.dot(all_heads[k * local_rows:(k + 1) * local_rows], my_weight, prefer...]
  transfers between devices with their start and end apart: 5 -> 18, of which waited for: 4 -> 10; matrix products, arithmetic and copies ran while one was open for 2% -> 9% of each run, Pallas kernels for 42% -> 43%
where the time goes in v2:
time: 235 us; the launch traced here: 234 us
  Pallas kernels  100 us (43%)
  waiting for transfers between devices  53.3 us (23%)
  starting transfers between devices  34.5 us (15%)
  local copies, waits for them, and re-layouts  16 us (7%)
  between operations  14.4 us (6%)
  matrix products  10 us (4%)
  other arithmetic  5.93 us (3%)
    pallas_call x2, Pallas kernels, attend(): pl.pallas_call(attend_kernel, out_shape=jax.ShapeDtypeStruct((local_rows,...  100 us
    ppermute x12, waiting for transfers between devices, within_group(): return lax.ppermute(x, 'seq', pairs)  47.6 us
    ppermute x12, starting transfers between devices, within_group(): return lax.ppermute(x, 'seq', pairs)  22.8 us
    ppermute x3, starting transfers between devices, passed_along(): return lax.ppermute(x, axis, pairs)  11.7 us
    dot_general x4, matrix products, on_device(): jnp.dot(all_heads[k * local_rows:(k + 1) * local_rows], my_weight, prefer...  10 us
    unnamed x16, local copies, waits for them, and re-layouts  6.26 us
  transfers between devices with their start and end apart: 18, of which 10 were waited for; matrix products, arithmetic and copies ran while one was open for 9% of the time, Pallas kernels for 43%

profile of v2, /device:TPU:0, one launch (start us, length us, event | category | flops | bytes accessed | tf_op | source)
XLA Modules:
  0.0 234.4 jit_solution(5953174116684072047)
XLA Ops:
  7.2 0.0 all-gather.2.cloned.1.call-start
  7.2 1.0 constant_dynamic-update-slice_fusion.1
  8.2 1.0 constant_dynamic-update-slice_fusion
  9.2 4.9 %collective-permute-start.3 = (bf16[256,1024]{1,0:T(8,128)(2,1)S(1)}, bf16[256,1024]{1,0:T(8,128)(2,1)S(1)}, u32[]{:S(2)}, u32[]{:S(2)}) collective-permute-start(bf16[256,1024]{1,0:T(8,128)(2,1)S(1)} %constant_dynamic-update-slice_fusion), channel_id=1, source_target_pairs={{0,4},{2,6},{4,8},{6,10},{8,12},{10,14},{12,16},{14,18},{16,20},{1... | collective-permute-start | bytes 1572872 | tf_op jit(solution)/shard_map/ppermute | solution.py:24
  14.1 4.2 %collective-permute-start.4 = (bf16[256,1024]{1,0:T(8,128)(2,1)S(1)}, bf16[256,1024]{1,0:T(8,128)(2,1)}, u32[]{:S(2)}, u32[]{:S(2)}) collective-permute-start(bf16[256,1024]{1,0:T(8,128)(2,1)S(1)} %constant_dynamic-update-slice_fusion), channel_id=1, source_target_pairs={{0,2},{2,4},{4,6},{6,8},{8,10},{10,12},{12,14},{14,16},{16,18},{18... | collective-permute-start | bytes 1572872 | tf_op jit(solution)/shard_map/ppermute | solution.py:24
  18.3 1.0 constant_dynamic-update-slice_fusion.3
  19.3 1.0 constant_dynamic-update-slice_fusion.2
  20.3 2.6 %collective-permute-start.5 = (bf16[32,1024]{1,0:T(8,128)(2,1)S(1)}, bf16[32,1024]{1,0:T(8,128)(2,1)S(1)}, u32[]{:S(2)}, u32[]{:S(2)}) collective-permute-start(bf16[32,1024]{1,0:T(8,128)(2,1)S(1)} %slice.42), channel_id=1, source_target_pairs={{0,2},{2,4},{4,6},{6,8},{8,10},{10,12},{12,14},{14,16},{16,18},{18... | collective-permute-start | bytes 196616 | tf_op jit(solution)/shard_map/ppermute | solution.py:24
  22.9 0.1 broadcast_in_dim.17
  23.0 2.1 constant_dynamic-slice_fusion
  25.1 1.5 collective-permute-start
  26.6 1.5 collective-permute-start.1
  28.2 3.1 %collective-permute-done.5 = bf16[32,1024]{1,0:T(8,128)(2,1)S(1)} collective-permute-done((bf16[32,1024]{1,0:T(8,128)(2,1)S(1)}, bf16[32,1024]{1,0:T(8,128)(2,1)S(1)}, u32[]{:S(2)}, u32[]{:S(2)}) %collective-permute-start.5) | collective-permute-done | bytes 65568 | tf_op jit(solution)/shard_map/ppermute | solution.py:24
  31.2 9.1 %collective-permute-start.2 = (bf16[128,1024]{1,0:T(8,128)(2,1)}, bf16[128,1024]{1,0:T(8,128)(2,1)S(1)}, u32[]{:S(2)}, u32[]{:S(2)}) collective-permute-start(bf16[128,1024]{1,0:T(8,128)(2,1)} %get-tuple-element.14), channel_id=1, source_target_pairs={{0,6},{2,0},{4,2},{6,4},{8,14},{10,8},{12,10},{14,12},{16,22},{18,... | collective-permute-start | bytes 786440 | tf_op jit(solution)/shard_map/ppermute | solution.py:163
  40.4 0.1 maximum_convert_fusion
  40.5 0.1 fusion.6
  40.6 0.0 collective-permute-done
  40.6 1.0 constant_dynamic-update-slice_fusion.13
  41.6 7.6 %collective-permute-done.1 = bf16[128,1024]{1,0:T(8,128)(2,1)S(1)} collective-permute-done((bf16[128,1024]{1,0:T(8,128)(2,1)}, bf16[128,1024]{1,0:T(8,128)(2,1)S(1)}, u32[]{:S(2)}, u32[]{:S(2)}) %collective-permute-start.1) | collective-permute-done | bytes 262176 | tf_op jit(solution)/shard_map/ppermute | solution.py:163
  49.2 0.0 collective-permute-done.2
  49.3 0.0 copy-start.4
  49.3 1.0 copy-done.4
  50.2 0.0 all-gather.2.cloned.1.call-update
  50.3 0.0 copy-start
  50.3 0.0 collective-permute-done.3
  50.3 0.0 collective-permute-done.4
  50.3 1.4 maximum_maximum_fusion
  51.7 0.1 fusion.5
  51.9 50.1 %shard_map.77 = bf16[256,512]{1,0:T(8,128)(2,1)S(1)} custom-call(s32[1]{0:T(128)} %bitcast.first_ref, bf16[256,1024]{1,0:T(8,128)(2,1)S(1)} %copy-done, bf16[896,512]{1,0:T(8,128)(2,1)S(1)} %get-tuple-element.7.k_ref, bf16[896,512]{1,0:T(8,128)(2,1)S(1)} %get-tuple-element.6.v_ref, f32[288,512]{1,0:T(8,128)S(1)} %get-tuple-element.9.k2_ref, ...), custom_call_target="tpu_custom_call" | custom-call | flops 25769803776 | bytes 8388608 | tf_op jit(solution)/shard_map/pallas_call | solution.py:139
  102.0 0.1 collective-permute-start.6
  102.0 1.4 collective-permute-start.7
  103.5 2.8 %collective-permute-start.8 = (bf16[256,512]{1,0:T(8,128)(2,1)S(1)}, bf16[256,512]{1,0:T(8,128)(2,1)}, u32[]{:S(2)}, u32[]{:S(2)}) collective-permute-start(bf16[256,512]{1,0:T(8,128)(2,1)S(1)} %shard_map.77), channel_id=1, source_target_pairs={{0,6},{2,0},{4,2},{6,4},{8,14},{10,8},{12,10},{14,12},{16,22},{18,... | collective-permute-start | bytes 786440 | tf_op jit(solution)/shard_map/ppermute | solution.py:163
  106.3 5.8 %collective-permute-done.6 = bf16[256,512]{1,0:T(8,128)(2,1)S(1)} collective-permute-done((bf16[256,512]{1,0:T(8,128)(2,1)S(1)}, bf16[256,512]{1,0:T(8,128)(2,1)S(1)}, u32[]{:S(2)}, u32[]{:S(2)}) %collective-permute-start.6) | collective-permute-done | bytes 262176 | tf_op jit(solution)/shard_map/ppermute | solution.py:163
  112.2 2.8 %collective-permute-done.7 = bf16[256,512]{1,0:T(8,128)(2,1)} collective-permute-done((bf16[256,512]{1,0:T(8,128)(2,1)S(1)}, bf16[256,512]{1,0:T(8,128)(2,1)}, u32[]{:S(2)}, u32[]{:S(2)}) %collective-permute-start.7) | collective-permute-done | bytes 262176 | tf_op jit(solution)/shard_map/ppermute | solution.py:163
  115.0 0.8 collective-permute-done.8
  115.8 0.5 broadcast_in_dim.20
  116.3 2.3 pad_maximum_fusion
  118.6 2.0 copy-done.2
  120.6 0.0 collective-permute-start.9
  120.6 50.1 %shard_map.78 = bf16[256,512]{1,0:T(8,128)(2,1)S(1)} custom-call(s32[1]{0:T(128)} %bitcast.first_ref, bf16[256,1024]{1,0:T(8,128)(2,1)S(1)} %copy-done.1, bf16[896,512]{1,0:T(8,128)(2,1)S(1)} %get-tuple-element.7.k_ref, bf16[896,512]{1,0:T(8,128)(2,1)S(1)} %get-tuple-element.6.v_ref, f32[288,512]{1,0:T(8,128)S(1)} %get-tuple-element.9.k2_ref, ...), custom_call_target="tpu_custom_call" | custom-call | flops 25769803776 | bytes 8388608 | tf_op jit(solution)/shard_map/pallas_call | solution.py:139
  170.8 0.7 collective-permute-start.10
  171.5 0.6 collective-permute-start.11
  172.2 1.6 collective-permute-start.12
  173.7 2.3 constant_dynamic-update-slice_fusion.9
  176.1 4.8 %collective-permute-done.10 = bf16[256,512]{1,0:T(8,128)(2,1)S(1)} collective-permute-done((bf16[256,512]{1,0:T(8,128)(2,1)S(1)}, bf16[256,512]{1,0:T(8,128)(2,1)S(1)}, u32[]{:S(2)}, u32[]{:S(2)}) %collective-permute-start.10) | collective-permute-done | bytes 262176 | tf_op jit(solution)/shard_map/ppermute | solution.py:163
  180.9 4.7 %collective-permute-done.11 = bf16[256,512]{1,0:T(8,128)(2,1)S(1)} collective-permute-done((bf16[256,512]{1,0:T(8,128)(2,1)S(1)}, bf16[256,512]{1,0:T(8,128)(2,1)S(1)}, u32[]{:S(2)}, u32[]{:S(2)}) %collective-permute-start.11) | collective-permute-done | bytes 262176 | tf_op jit(solution)/shard_map/ppermute | solution.py:163
  185.6 1.2 pad_maximum_fusion.1
  186.8 2.7 %collective-permute-done.13 = bf16[1024,512]{1,0:T(8,128)(2,1)S(1)} collective-permute-done((bf16[1024,512]{1,0:T(8,128)(2,1)S(1)}, bf16[1024,512]{1,0:T(8,128)(2,1)S(1)}, u32[]{:S(2)}, u32[]{:S(2)}) %collective-permute-start.13) | collective-permute-done | bytes 1048608 | tf_op jit(solution)/shard_map/ppermute | solution.py:230
  189.4 1.1 constant_dynamic-update-slice_fusion.7
  190.5 3.9 %convolution_convert_fusion.2 = bf16[256,1024]{1,0:T(8,128)(2,1)S(1)} fusion(bf16[2048,1024]{1,0:T(8,128)(2,1)} %all-gather.2.cloned.1.call-done, bf16[1024,2048]{1,0:T(8,128)(2,1)} %constant_dynamic-update-slice_fusion.7), kind=kOutput, calls=%fused_computation.4 | convolution fusion | flops 1074003968 | bytes 5767168 | tf_op jit(solution)/shard_map/dot_general | solution.py:237
  194.5 1.1 collective-permute-start.15
  195.6 3.6 %convolution_convert_fusion.3 = bf16[256,1024]{1,0:T(8,128)(2,1)S(1)} fusion(bf16[2048,1024]{1,0:T(8,128)(2,1)} %all-gather.2.cloned.1.call-done, bf16[1024,2048]{1,0:T(8,128)(2,1)S(1)} %copy-done.3), kind=kOutput, calls=%fused_computation.5 | convolution fusion | flops 1074003968 | bytes 5767168 | tf_op jit(solution)/shard_map/dot_general | solution.py:237
  199.2 1.5 collective-permute-start.14
  200.7 1.3 convolution_convert_fusion.1
  202.0 0.6 collective-permute-start.16
  202.6 0.9 pad_maximum_fusion.2
  203.5 10.5 %collective-permute-done.14 = bf16[256,1024]{1,0:T(8,128)(2,1)S(1)} collective-permute-done((bf16[256,1024]{1,0:T(8,128)(2,1)S(1)}, bf16[256,1024]{1,0:T(8,128)(2,1)S(1)}, u32[]{:S(2)}, u32[]{:S(2)}) %collective-permute-start.14) | collective-permute-done | bytes 524320 | tf_op jit(solution)/shard_map/ppermute | solution.py:163
  214.0 0.2 broadcast_in_dim.19
  214.2 0.1 constant_dynamic-update-slice_fusion.6
  214.3 0.1 constant_dynamic-update-slice_fusion.5
  214.4 10.5 %collective-permute-done.16 = bf16[256,1024]{1,0:T(8,128)(2,1)S(1)} collective-permute-done((bf16[256,1024]{1,0:T(8,128)(2,1)S(1)}, bf16[256,1024]{1,0:T(8,128)(2,1)S(1)}, u32[]{:S(2)}, u32[]{:S(2)}) %collective-permute-start.16) | collective-permute-done | bytes 524320 | tf_op jit(solution)/shard_map/ppermute | solution.py:163
  224.9 1.3 fusion
  226.2 0.0 copy-start.5
  226.2 1.3 copy-done.5
  (19 shorter events, 0.1 us)
Async XLA Ops:
  7.2 183.4 %all-gather.2.cloned.1.call-start = ((), (), s32[]{:S(2)}) async-start(), calls=%async_computation | async-start | bytes 5242880 | tf_op jit(solution)/shard_map/all_gather | solution.py:200
  9.2 41.1 %collective-permute-start.3 = (bf16[256,1024]{1,0:T(8,128)(2,1)S(1)}, bf16[256,1024]{1,0:T(8,128)(2,1)S(1)}, u32[]{:S(2)}, u32[]{:S(2)}) collective-permute-start(bf16[256,1024]{1,0:T(8,128)(2,1)S(1)} %constant_dynamic-update-slice_fusion), channel_id=1, source_target_pairs={{0,4},{2,6},{4,8},{6,10},{8,12},{10,14},{12,16},{14,18},{16,20},{1... | collective-permute-start | bytes 1572872 | tf_op jit(solution)/shard_map/ppermute | solution.py:24
  14.1 36.2 %collective-permute-start.4 = (bf16[256,1024]{1,0:T(8,128)(2,1)S(1)}, bf16[256,1024]{1,0:T(8,128)(2,1)}, u32[]{:S(2)}, u32[]{:S(2)}) collective-permute-start(bf16[256,1024]{1,0:T(8,128)(2,1)S(1)} %constant_dynamic-update-slice_fusion), channel_id=1, source_target_pairs={{0,2},{2,4},{4,6},{6,8},{8,10},{10,12},{12,14},{14,16},{16,18},{18... | collective-permute-start | bytes 1572872 | tf_op jit(solution)/shard_map/ppermute | solution.py:24
  20.3 11.0 %collective-permute-start.5 = (bf16[32,1024]{1,0:T(8,128)(2,1)S(1)}, bf16[32,1024]{1,0:T(8,128)(2,1)S(1)}, u32[]{:S(2)}, u32[]{:S(2)}) collective-permute-start(bf16[32,1024]{1,0:T(8,128)(2,1)S(1)} %slice.42), channel_id=1, source_target_pairs={{0,2},{2,4},{4,6},{6,8},{8,10},{10,12},{12,14},{14,16},{16,18},{18... | collective-permute-start | bytes 196616 | tf_op jit(solution)/shard_map/ppermute | solution.py:24
  25.1 15.5 %collective-permute-start = (bf16[128,1024]{1,0:T(8,128)(2,1)}, bf16[128,1024]{1,0:T(8,128)(2,1)}, u32[]{:S(2)}, u32[]{:S(2)}) collective-permute-start(bf16[128,1024]{1,0:T(8,128)(2,1)} %get-tuple-element.15), channel_id=1, source_target_pairs={{0,2},{2,4},{4,6},{6,0},{8,10},{10,12},{12,14},{14,8},{16,18},{18,... | collective-permute-start | bytes 786440 | tf_op jit(solution)/shard_map/ppermute | solution.py:163
  26.6 22.6 %collective-permute-start.1 = (bf16[128,1024]{1,0:T(8,128)(2,1)}, bf16[128,1024]{1,0:T(8,128)(2,1)S(1)}, u32[]{:S(2)}, u32[]{:S(2)}) collective-permute-start(bf16[128,1024]{1,0:T(8,128)(2,1)} %get-tuple-element.17), channel_id=1, source_target_pairs={{0,4},{2,6},{4,0},{6,2},{8,12},{10,14},{12,8},{14,10},{16,20},{18,... | collective-permute-start | bytes 786440 | tf_op jit(solution)/shard_map/ppermute | solution.py:163
  31.2 18.0 %collective-permute-start.2 = (bf16[128,1024]{1,0:T(8,128)(2,1)}, bf16[128,1024]{1,0:T(8,128)(2,1)S(1)}, u32[]{:S(2)}, u32[]{:S(2)}) collective-permute-start(bf16[128,1024]{1,0:T(8,128)(2,1)} %get-tuple-element.14), channel_id=1, source_target_pairs={{0,6},{2,0},{4,2},{6,4},{8,14},{10,8},{12,10},{14,12},{16,22},{18,... | collective-permute-start | bytes 786440 | tf_op jit(solution)/shard_map/ppermute | solution.py:163
  49.3 1.0 copy-start.4
  50.3 1.6 copy-start
  102.0 10.2 %collective-permute-start.6 = (bf16[256,512]{1,0:T(8,128)(2,1)S(1)}, bf16[256,512]{1,0:T(8,128)(2,1)S(1)}, u32[]{:S(2)}, u32[]{:S(2)}) collective-permute-start(bf16[256,512]{1,0:T(8,128)(2,1)S(1)} %shard_map.77), channel_id=1, source_target_pairs={{0,2},{2,4},{4,6},{6,0},{8,10},{10,12},{12,14},{14,8},{16,18},{18,... | collective-permute-start | bytes 786440 | tf_op jit(solution)/shard_map/ppermute | solution.py:163
  102.0 12.9 %collective-permute-start.7 = (bf16[256,512]{1,0:T(8,128)(2,1)S(1)}, bf16[256,512]{1,0:T(8,128)(2,1)}, u32[]{:S(2)}, u32[]{:S(2)}) collective-permute-start(bf16[256,512]{1,0:T(8,128)(2,1)S(1)} %shard_map.77), channel_id=1, source_target_pairs={{0,4},{2,6},{4,0},{6,2},{8,12},{10,14},{12,8},{14,10},{16,20},{18,... | collective-permute-start | bytes 786440 | tf_op jit(solution)/shard_map/ppermute | solution.py:163
  103.5 12.3 %collective-permute-start.8 = (bf16[256,512]{1,0:T(8,128)(2,1)S(1)}, bf16[256,512]{1,0:T(8,128)(2,1)}, u32[]{:S(2)}, u32[]{:S(2)}) collective-permute-start(bf16[256,512]{1,0:T(8,128)(2,1)S(1)} %shard_map.77), channel_id=1, source_target_pairs={{0,6},{2,0},{4,2},{6,4},{8,14},{10,8},{12,10},{14,12},{16,22},{18,... | collective-permute-start | bytes 786440 | tf_op jit(solution)/shard_map/ppermute | solution.py:163
  106.3 14.3 %copy-start.1 = (bf16[256,1024]{1,0:T(8,128)(2,1)S(1)}, bf16[256,1024]{1,0:T(8,128)(2,1)}, u32[]{:S(2)}) copy-start(bf16[256,1024]{1,0:T(8,128)(2,1)} %q_ref.1) | copy-start | bytes 1572868
  118.6 2.0 copy-start.2
  120.6 53.1 %collective-permute-start.9 = (bf16[1024,512]{1,0:T(8,128)(2,1)}, bf16[1024,512]{1,0:T(8,128)(2,1)}, u32[]{:S(2)}, u32[]{:S(2)}) collective-permute-start(bf16[1024,512]{1,0:T(8,128)(2,1)} %get-tuple-element.12), channel_id=1, source_target_pairs={{0,1},{1,0},{2,3},{3,2},{4,5},{5,4},{6,7},{7,6},{8,9},{9,8},{10,11... | collective-permute-start | bytes 3145736 | tf_op jit(solution)/shard_map/ppermute | solution.py:230
  170.8 10.1 %collective-permute-start.10 = (bf16[256,512]{1,0:T(8,128)(2,1)S(1)}, bf16[256,512]{1,0:T(8,128)(2,1)S(1)}, u32[]{:S(2)}, u32[]{:S(2)}) collective-permute-start(bf16[256,512]{1,0:T(8,128)(2,1)S(1)} %shard_map.78), channel_id=1, source_target_pairs={{0,2},{2,4},{4,6},{6,0},{8,10},{10,12},{12,14},{14,8},{16,18},{18,... | collective-permute-start | bytes 786440 | tf_op jit(solution)/shard_map/ppermute | solution.py:163
  171.5 14.1 %collective-permute-start.11 = (bf16[256,512]{1,0:T(8,128)(2,1)S(1)}, bf16[256,512]{1,0:T(8,128)(2,1)S(1)}, u32[]{:S(2)}, u32[]{:S(2)}) collective-permute-start(bf16[256,512]{1,0:T(8,128)(2,1)S(1)} %shard_map.78), channel_id=1, source_target_pairs={{0,4},{2,6},{4,0},{6,2},{8,12},{10,14},{12,8},{14,10},{16,20},{18,... | collective-permute-start | bytes 786440 | tf_op jit(solution)/shard_map/ppermute | solution.py:163
  172.2 13.4 %collective-permute-start.12 = (bf16[256,512]{1,0:T(8,128)(2,1)S(1)}, bf16[256,512]{1,0:T(8,128)(2,1)S(1)}, u32[]{:S(2)}, u32[]{:S(2)}) collective-permute-start(bf16[256,512]{1,0:T(8,128)(2,1)S(1)} %shard_map.78), channel_id=1, source_target_pairs={{0,6},{2,0},{4,2},{6,4},{8,14},{10,8},{12,10},{14,12},{16,22},{18,... | collective-permute-start | bytes 786440 | tf_op jit(solution)/shard_map/ppermute | solution.py:163
  186.8 2.7 %collective-permute-start.13 = (bf16[1024,512]{1,0:T(8,128)(2,1)S(1)}, bf16[1024,512]{1,0:T(8,128)(2,1)S(1)}, u32[]{:S(2)}, u32[]{:S(2)}) collective-permute-start(bf16[1024,512]{1,0:T(8,128)(2,1)S(1)} %get-tuple-element.10), channel_id=1, source_target_pairs={{0,1},{1,0},{2,3},{3,2},{4,5},{5,4},{6,7},{7,6},{8,9},{9,8},{10,11... | collective-permute-start | bytes 3145736 | tf_op jit(solution)/shard_map/ppermute | solution.py:230
  190.5 5.1 %copy-start.3 = (bf16[1024,2048]{1,0:T(8,128)(2,1)S(1)}, bf16[1024,2048]{1,0:T(8,128)(2,1)}, u32[]{:S(2)}) copy-start(bf16[1024,2048]{1,0:T(8,128)(2,1)} %constant_dynamic-update-slice_fusion.7) | copy-start | bytes 12582916
  194.5 6.3 %copy-start.6 = (bf16[2048,1024]{1,0:T(8,128)(2,1)S(1)}, bf16[2048,1024]{1,0:T(8,128)(2,1)}, u32[]{:S(2)}) copy-start(bf16[2048,1024]{1,0:T(8,128)(2,1)} %all-gather.2.cloned.1.call-done) | copy-start | bytes 12582916
  194.5 19.8 %collective-permute-start.15 = (bf16[256,1024]{1,0:T(8,128)(2,1)S(1)}, bf16[256,1024]{1,0:T(8,128)(2,1)S(1)}, u32[]{:S(2)}, u32[]{:S(2)}) collective-permute-start(bf16[256,1024]{1,0:T(8,128)(2,1)S(1)} %convolution_convert_fusion.2), channel_id=1, source_target_pairs={{0,4},{2,6},{4,0},{6,2},{8,12},{10,14},{12,8},{14,10},{16,20},{18,... | collective-permute-start | bytes 1572872 | tf_op jit(solution)/shard_map/ppermute | solution.py:163
  199.2 14.8 %collective-permute-start.14 = (bf16[256,1024]{1,0:T(8,128)(2,1)S(1)}, bf16[256,1024]{1,0:T(8,128)(2,1)S(1)}, u32[]{:S(2)}, u32[]{:S(2)}) collective-permute-start(bf16[256,1024]{1,0:T(8,128)(2,1)S(1)} %convolution_convert_fusion.3), channel_id=1, source_target_pairs={{0,6},{2,0},{4,2},{6,4},{8,14},{10,8},{12,10},{14,12},{16,22},{18,... | collective-permute-start | bytes 1572872 | tf_op jit(solution)/shard_map/ppermute | solution.py:163
  202.0 22.8 %collective-permute-start.16 = (bf16[256,1024]{1,0:T(8,128)(2,1)S(1)}, bf16[256,1024]{1,0:T(8,128)(2,1)S(1)}, u32[]{:S(2)}, u32[]{:S(2)}) collective-permute-start(bf16[256,1024]{1,0:T(8,128)(2,1)S(1)} %convolution_convert_fusion.1), channel_id=1, source_target_pairs={{0,2},{2,4},{4,6},{6,0},{8,10},{10,12},{12,14},{14,8},{16,18},{18,... | collective-permute-start | bytes 1572872 | tf_op jit(solution)/shard_map/ppermute | solution.py:163
  226.2 1.3 copy-start.5
Sparse Core Ops, SparseCore 0:
  50.4 81.9 all-gather.1

commit v3 on v2

--- a/solution.py
+++ b/solution.py
@@ -205,7 +205,7 @@
         axis_index_groups=[list(range(p, seq_size, group)) for p in range(group)],
     )
 
-    splits = math.gcd(2, width // HEAD_SIZE)
+    splits = 1
     split_columns = columns // splits
     all_heads = jnp.zeros((group * local_rows, heads * columns), jnp.bfloat16)
     attended = []

time: 235 us -> 237 us (level)
  waiting for transfers between devices: 53.3 us -> 59.3 us
  starting transfers between devices: 34.5 us -> 29.7 us
    ppermute x12 -> x9, starting transfers between devices: 22.8 us -> 17.9 us  [within_group(): return lax.ppermute(x, 'seq', pairs)]
    ppermute x12 -> x9, waiting for transfers between devices: 47.6 us -> 49.9 us  [within_group(): return lax.ppermute(x, 'seq', pairs)]
    pallas_call x2 -> x1, Pallas kernels: 100 us -> 101 us  [attend(): pl.pallas_call(attend_kernel, out_shape=jax.ShapeDtypeStruct((local_rows,...]
    unnamed x16 -> x18, local copies, waits for them, and re-layouts: 6.26 us -> 5.98 us
  transfers between devices with their start and end apart: 18 -> 14, of which waited for: 10 -> 7; matrix products, arithmetic and copies ran while one was open for 9% -> 9% of each run, Pallas kernels for 43% -> 43%
where the time goes in v3:
time: 237 us; the launch traced here: 236 us
  Pallas kernels  101 us (43%)
  waiting for transfers between devices  59.3 us (25%)
  starting transfers between devices  29.7 us (13%)
  local copies, waits for them, and re-layouts  15.3 us (6%)
  between operations  14.4 us (6%)
  matrix products  11.4 us (5%)
  other arithmetic  5.86 us (2%)
    pallas_call x1, Pallas kernels, attend(): pl.pallas_call(attend_kernel, out_shape=jax.ShapeDtypeStruct((local_rows,...  101 us
    ppermute x9, waiting for transfers between devices, within_group(): return lax.ppermute(x, 'seq', pairs)  49.9 us
    ppermute x9, starting transfers between devices, within_group(): return lax.ppermute(x, 'seq', pairs)  17.9 us
    ppermute x3, starting transfers between devices, passed_along(): return lax.ppermute(x, axis, pairs)  11.7 us
    dot_general x4, matrix products, on_device(): jnp.dot(all_heads[k * local_rows:(k + 1) * local_rows], my_weight, prefer...  11.4 us
    unnamed x18, local copies, waits for them, and re-layouts  5.98 us
    ppermute x3, waiting for transfers between devices, passed_along(): return lax.ppermute(x, axis, pairs)  5.02 us
  transfers between devices with their start and end apart: 14, of which 7 were waited for; matrix products, arithmetic and copies ran while one was open for 9% of the time, Pallas kernels for 43%

profile of v3, /device:TPU:0, one launch (start us, length us, event | category | flops | bytes accessed | tf_op | source)
XLA Modules:
  0.0 236.4 jit_solution(13033844504091835764)
XLA Ops:
  7.2 0.0 copy-start.3
  7.2 0.0 all-gather.2.cloned.1.call-start
  7.2 1.1 constant_dynamic-update-slice_fusion.1
  8.3 1.0 constant_dynamic-update-slice_fusion
  9.3 5.7 %collective-permute-start.3 = (bf16[256,1024]{1,0:T(8,128)(2,1)S(1)}, bf16[256,1024]{1,0:T(8,128)(2,1)}, u32[]{:S(2)}, u32[]{:S(2)}) collective-permute-start(bf16[256,1024]{1,0:T(8,128)(2,1)S(1)} %constant_dynamic-update-slice_fusion), channel_id=1, source_target_pairs={{0,4},{2,6},{4,8},{6,10},{8,12},{10,14},{12,16},{14,18},{16,20},{1... | collective-permute-start | bytes 1572872 | tf_op jit(solution)/shard_map/ppermute | solution.py:24
  14.9 4.2 %collective-permute-start.4 = (bf16[256,1024]{1,0:T(8,128)(2,1)S(1)}, bf16[256,1024]{1,0:T(8,128)(2,1)}, u32[]{:S(2)}, u32[]{:S(2)}) collective-permute-start(bf16[256,1024]{1,0:T(8,128)(2,1)S(1)} %constant_dynamic-update-slice_fusion), channel_id=1, source_target_pairs={{0,2},{2,4},{4,6},{6,8},{8,10},{10,12},{12,14},{14,16},{16,18},{18... | collective-permute-start | bytes 1572872 | tf_op jit(solution)/shard_map/ppermute | solution.py:24
  19.1 1.0 constant_dynamic-update-slice_fusion.3
  20.1 1.0 constant_dynamic-update-slice_fusion.2
  21.1 1.8 collective-permute-start.5
  23.0 0.1 broadcast_in_dim.16
  23.1 0.0 copy-done.3
  23.1 0.9 constant_dynamic-slice_fusion
  24.0 1.5 collective-permute-start
  25.5 1.5 collective-permute-start.1
  27.1 5.0 %collective-permute-done.5 = bf16[32,1024]{1,0:T(8,128)(2,1)S(1)} collective-permute-done((bf16[32,1024]{1,0:T(8,128)(2,1)S(1)}, bf16[32,1024]{1,0:T(8,128)(2,1)S(1)}, u32[]{:S(2)}, u32[]{:S(2)}) %collective-permute-start.5) | collective-permute-done | bytes 65568 | tf_op jit(solution)/shard_map/ppermute | solution.py:24
  32.1 8.3 %collective-permute-start.2 = (bf16[128,1024]{1,0:T(8,128)(2,1)}, bf16[128,1024]{1,0:T(8,128)(2,1)S(1)}, u32[]{:S(2)}, u32[]{:S(2)}) collective-permute-start(bf16[128,1024]{1,0:T(8,128)(2,1)} %get-tuple-element.12), channel_id=1, source_target_pairs={{0,6},{2,0},{4,2},{6,4},{8,14},{10,8},{12,10},{14,12},{16,22},{18,... | collective-permute-start | bytes 786440 | tf_op jit(solution)/shard_map/ppermute | solution.py:163
  40.4 0.1 maximum_convert_fusion
  40.5 0.1 fusion.6
  40.6 0.0 collective-permute-done
  40.7 8.6 %collective-permute-done.1 = bf16[128,1024]{1,0:T(8,128)(2,1)S(1)} collective-permute-done((bf16[128,1024]{1,0:T(8,128)(2,1)}, bf16[128,1024]{1,0:T(8,128)(2,1)S(1)}, u32[]{:S(2)}, u32[]{:S(2)}) %collective-permute-start.1) | collective-permute-done | bytes 262176 | tf_op jit(solution)/shard_map/ppermute | solution.py:163
  49.3 0.0 collective-permute-done.2
  49.4 0.0 copy-start.1
  49.4 1.0 copy-done.1
  50.3 0.0 all-gather.2.cloned.1.call-update
  50.4 0.0 copy-start
  50.4 0.0 collective-permute-done.3
  50.4 0.0 collective-permute-done.4
  50.4 1.6 maximum_maximum_fusion
  52.0 0.1 fusion.5
  52.1 0.0 copy-done
  52.1 100.5 %shard_map.77 = bf16[256,1024]{1,0:T(8,128)(2,1)} custom-call(s32[1]{0:T(128)} %bitcast.first_ref, bf16[256,1024]{1,0:T(8,128)(2,1)S(1)} %copy-done, bf16[896,512]{1,0:T(8,128)(2,1)S(1)} %get-tuple-element.9.k_ref, bf16[896,512]{1,0:T(8,128)(2,1)S(1)} %get-tuple-element.8.v_ref, f32[288,512]{1,0:T(8,128)S(1)} %get-tuple-element.11.k2_ref, ...), custom_call_target="tpu_custom_call" | custom-call | flops 51539607552 | bytes 8388608 | tf_op jit(solution)/shard_map/pallas_call | solution.py:139
  152.6 0.0 copy-start.4
  152.6 0.0 collective-permute-start.6
  152.6 0.3 collective-permute-start.7
  152.9 2.9 %collective-permute-start.8 = (bf16[256,1024]{1,0:T(8,128)(2,1)}, bf16[256,1024]{1,0:T(8,128)(2,1)S(1)}, u32[]{:S(2)}, u32[]{:S(2)}) collective-permute-start(bf16[256,1024]{1,0:T(8,128)(2,1)} %shard_map.77), channel_id=1, source_target_pairs={{0,6},{2,0},{4,2},{6,4},{8,14},{10,8},{12,10},{14,12},{16,22},{18,... | collective-permute-start | bytes 1572872 | tf_op jit(solution)/shard_map/ppermute | solution.py:163
  155.9 12.8 %collective-permute-done.6 = bf16[256,1024]{1,0:T(8,128)(2,1)S(1)} collective-permute-done((bf16[256,1024]{1,0:T(8,128)(2,1)}, bf16[256,1024]{1,0:T(8,128)(2,1)S(1)}, u32[]{:S(2)}, u32[]{:S(2)}) %collective-permute-start.6) | collective-permute-done | bytes 524320 | tf_op jit(solution)/shard_map/ppermute | solution.py:163
  168.6 8.3 %collective-permute-done.7 = bf16[256,1024]{1,0:T(8,128)(2,1)S(1)} collective-permute-done((bf16[256,1024]{1,0:T(8,128)(2,1)}, bf16[256,1024]{1,0:T(8,128)(2,1)S(1)}, u32[]{:S(2)}, u32[]{:S(2)}) %collective-permute-start.7) | collective-permute-done | bytes 524320 | tf_op jit(solution)/shard_map/ppermute | solution.py:163
  176.9 0.0 copy-start.5
  176.9 0.0 collective-permute-done.8
  176.9 0.8 copy-done.5
  177.7 0.9 copy-done.6
  178.5 2.5 %broadcast_in_dim.19 = bf16[1024,2048]{1,0:T(8,128)(2,1)} broadcast(bf16[]{:T(256)} %constant.54.clone.1), dimensions={} | broadcast | bytes 4194306 | tf_op jit(solution)/shard_map/broadcast_in_dim | solution.py:210
  181.1 0.0 copy-done.4
  181.1 4.1 %pad_maximum_fusion = (bf16[1024,1024]{1,0:T(8,128)(2,1)S(1)}, bf16[1024,2048]{1,0:T(8,128)(2,1)}) fusion(bf16[256,1024]{1,0:T(8,128)(2,1)} %copy-done.6, bf16[256,1024]{1,0:T(8,128)(2,1)} %copy-done.5, bf16[256,1024]{1,0:T(8,128)(2,1)S(1)} %collective-permute-done.6, bf16[256,1024]{1,0:T(8,128)(2,1)S(1)} %copy-done.4, bf16[1024,2048]{1,0:T(8,128)(2,1)} %broadcast_in_dim.19, ...), kind=kLoop, calls=%fused_computation | loop fusion | flops 8388608 | bytes 6291460 | tf_op jit(solution)/shard_map/concatenate | solution.py:224
  185.2 0.0 collective-permute-start.9
  185.2 4.3 %collective-permute-done.9 = bf16[1024,1024]{1,0:T(8,128)(2,1)} collective-permute-done((bf16[1024,1024]{1,0:T(8,128)(2,1)S(1)}, bf16[1024,1024]{1,0:T(8,128)(2,1)}, u32[]{:S(2)}, u32[]{:S(2)}) %collective-permute-start.9) | collective-permute-done | bytes 2097184 | tf_op jit(solution)/shard_map/ppermute | solution.py:230
  189.5 3.1 %constant_dynamic-update-slice_fusion.7 = bf16[1024,2048]{1,0:T(8,128)(2,1)} fusion(bf16[1024,2048]{1,0:T(8,128)(2,1)} %get-tuple-element.7, bf16[1024,1024]{1,0:T(8,128)(2,1)} %collective-permute-done.9, s32[]{:T(128)S(6)} %select_n.43), kind=kLoop, calls=%fused_computation.20 | loop fusion | bytes 4194308 | tf_op jit(solution)/shard_map/dynamic_update_slice | solution.py:232
  192.7 0.0 all-gather.2.cloned.1.call-done
  192.7 0.0 copy-start.7
  192.7 3.9 %convolution_convert_fusion.2 = bf16[256,1024]{1,0:T(8,128)(2,1)S(1)} fusion(bf16[2048,1024]{1,0:T(8,128)(2,1)} %all-gather.2.cloned.1.call-done, bf16[1024,2048]{1,0:T(8,128)(2,1)} %constant_dynamic-update-slice_fusion.7), kind=kOutput, calls=%fused_computation.5 | convolution fusion | flops 1074003968 | bytes 5767168 | tf_op jit(solution)/shard_map/dot_general | solution.py:237
  196.6 0.8 collective-permute-start.11
  197.4 0.0 copy-done.7
  197.4 2.5 %convolution_convert_fusion.3 = bf16[256,1024]{1,0:T(8,128)(2,1)S(1)} fusion(bf16[2048,1024]{1,0:T(8,128)(2,1)S(1)} %copy-done.7, bf16[1024,2048]{1,0:T(8,128)(2,1)} %constant_dynamic-update-slice_fusion.7), kind=kOutput, calls=%fused_computation.6 | convolution fusion | flops 1074003968 | bytes 5767168 | tf_op jit(solution)/shard_map/dot_general | solution.py:237
  199.9 2.3 collective-permute-start.10
  202.2 2.5 %convolution_convert_fusion.1 = bf16[256,1024]{1,0:T(8,128)(2,1)S(1)} fusion(bf16[2048,1024]{1,0:T(8,128)(2,1)S(1)} %copy-done.7, bf16[1024,2048]{1,0:T(8,128)(2,1)} %constant_dynamic-update-slice_fusion.7), kind=kOutput, calls=%fused_computation.4 | convolution fusion | flops 1074003968 | bytes 5767168 | tf_op jit(solution)/shard_map/dot_general | solution.py:237
  204.7 0.3 collective-permute-start.12
  205.0 10.2 %collective-permute-done.10 = bf16[256,1024]{1,0:T(8,128)(2,1)S(1)} collective-permute-done((bf16[256,1024]{1,0:T(8,128)(2,1)S(1)}, bf16[256,1024]{1,0:T(8,128)(2,1)S(1)}, u32[]{:S(2)}, u32[]{:S(2)}) %collective-permute-start.10) | collective-permute-done | bytes 524320 | tf_op jit(solution)/shard_map/ppermute | solution.py:163
  215.2 0.2 broadcast_in_dim.18
  215.4 0.1 constant_dynamic-update-slice_fusion.6
  215.5 0.0 collective-permute-done.11
  215.5 10.1 %collective-permute-done.12 = bf16[256,1024]{1,0:T(8,128)(2,1)S(1)} collective-permute-done((bf16[256,1024]{1,0:T(8,128)(2,1)S(1)}, bf16[256,1024]{1,0:T(8,128)(2,1)S(1)}, u32[]{:S(2)}, u32[]{:S(2)}) %collective-permute-start.12) | collective-permute-done | bytes 524320 | tf_op jit(solution)/shard_map/ppermute | solution.py:163
  225.7 2.5 %fusion = bf16[256,4096]{1,0:T(8,128)(2,1)S(1)} fusion(bf16[256,4096]{1,0:T(8,128)(2,1)S(1)} %constant_dynamic-update-slice_fusion.4, s32[]{:T(128)S(6)} %select_n.34, bf16[2048,1024]{1,0:T(8,128)(2,1)S(1)} %copy-done.7, bf16[1024,2048]{1,0:T(8,128)(2,1)} %constant_dynamic-update-slice_fusion.7), kind=kOutput, calls=%fused_computation.3 | convolution fusion | flops 1074003968 | bytes 5767172 | tf_op jit(solution)/shard_map/dot_general | solution.py:237
  228.2 0.0 copy-start.2
  228.2 1.3 copy-done.2
  (9 shorter events, 0.2 us)
Async XLA Ops:
  7.2 16.0 %copy-start.3 = (bf16[128,4096]{1,0:T(8,128)(2,1)S(1)}, bf16[128,4096]{1,0:T(8,128)(2,1)}, u32[]{:S(2)}) copy-start(bf16[128,4096]{1,0:T(8,128)(2,1)} %param.11) | copy-start | bytes 3145732
  7.2 185.5 %all-gather.2.cloned.1.call-start = ((), (), s32[]{:S(2)}) async-start(), calls=%async_computation | async-start | bytes 5242880 | tf_op jit(solution)/shard_map/all_gather | solution.py:200
  9.3 41.1 %collective-permute-start.3 = (bf16[256,1024]{1,0:T(8,128)(2,1)S(1)}, bf16[256,1024]{1,0:T(8,128)(2,1)}, u32[]{:S(2)}, u32[]{:S(2)}) collective-permute-start(bf16[256,1024]{1,0:T(8,128)(2,1)S(1)} %constant_dynamic-update-slice_fusion), channel_id=1, source_target_pairs={{0,4},{2,6},{4,8},{6,10},{8,12},{10,14},{12,16},{14,18},{16,20},{1... | collective-permute-start | bytes 1572872 | tf_op jit(solution)/shard_map/ppermute | solution.py:24
  14.9 35.4 %collective-permute-start.4 = (bf16[256,1024]{1,0:T(8,128)(2,1)S(1)}, bf16[256,1024]{1,0:T(8,128)(2,1)}, u32[]{:S(2)}, u32[]{:S(2)}) collective-permute-start(bf16[256,1024]{1,0:T(8,128)(2,1)S(1)} %constant_dynamic-update-slice_fusion), channel_id=1, source_target_pairs={{0,2},{2,4},{4,6},{6,8},{8,10},{10,12},{12,14},{14,16},{16,18},{18... | collective-permute-start | bytes 1572872 | tf_op jit(solution)/shard_map/ppermute | solution.py:24
  21.1 11.0 %collective-permute-start.5 = (bf16[32,1024]{1,0:T(8,128)(2,1)S(1)}, bf16[32,1024]{1,0:T(8,128)(2,1)S(1)}, u32[]{:S(2)}, u32[]{:S(2)}) collective-permute-start(bf16[32,1024]{1,0:T(8,128)(2,1)S(1)} %slice.38), channel_id=1, source_target_pairs={{0,2},{2,4},{4,6},{6,8},{8,10},{10,12},{12,14},{14,16},{16,18},{18... | collective-permute-start | bytes 196616 | tf_op jit(solution)/shard_map/ppermute | solution.py:24
  24.0 16.6 %collective-permute-start = (bf16[128,1024]{1,0:T(8,128)(2,1)}, bf16[128,1024]{1,0:T(8,128)(2,1)S(1)}, u32[]{:S(2)}, u32[]{:S(2)}) collective-permute-start(bf16[128,1024]{1,0:T(8,128)(2,1)} %get-tuple-element.13), channel_id=1, source_target_pairs={{0,2},{2,4},{4,6},{6,0},{8,10},{10,12},{12,14},{14,8},{16,18},{18,... | collective-permute-start | bytes 786440 | tf_op jit(solution)/shard_map/ppermute | solution.py:163
  25.5 23.7 %collective-permute-start.1 = (bf16[128,1024]{1,0:T(8,128)(2,1)}, bf16[128,1024]{1,0:T(8,128)(2,1)S(1)}, u32[]{:S(2)}, u32[]{:S(2)}) collective-permute-start(bf16[128,1024]{1,0:T(8,128)(2,1)} %get-tuple-element.15), channel_id=1, source_target_pairs={{0,4},{2,6},{4,0},{6,2},{8,12},{10,14},{12,8},{14,10},{16,20},{18,... | collective-permute-start | bytes 786440 | tf_op jit(solution)/shard_map/ppermute | solution.py:163
  32.1 17.2 %collective-permute-start.2 = (bf16[128,1024]{1,0:T(8,128)(2,1)}, bf16[128,1024]{1,0:T(8,128)(2,1)S(1)}, u32[]{:S(2)}, u32[]{:S(2)}) collective-permute-start(bf16[128,1024]{1,0:T(8,128)(2,1)} %get-tuple-element.12), channel_id=1, source_target_pairs={{0,6},{2,0},{4,2},{6,4},{8,14},{10,8},{12,10},{14,12},{16,22},{18,... | collective-permute-start | bytes 786440 | tf_op jit(solution)/shard_map/ppermute | solution.py:163
  49.4 1.0 copy-start.1
  50.4 1.8 copy-start
  152.6 28.5 %copy-start.4 = (bf16[256,1024]{1,0:T(8,128)(2,1)S(1)}, bf16[256,1024]{1,0:T(8,128)(2,1)}, u32[]{:S(2)}) copy-start(bf16[256,1024]{1,0:T(8,128)(2,1)} %shard_map.77) | copy-start | bytes 1572868
  152.6 16.0 %collective-permute-start.6 = (bf16[256,1024]{1,0:T(8,128)(2,1)}, bf16[256,1024]{1,0:T(8,128)(2,1)S(1)}, u32[]{:S(2)}, u32[]{:S(2)}) collective-permute-start(bf16[256,1024]{1,0:T(8,128)(2,1)} %shard_map.77), channel_id=1, source_target_pairs={{0,2},{2,4},{4,6},{6,0},{8,10},{10,12},{12,14},{14,8},{16,18},{18,... | collective-permute-start | bytes 1572872 | tf_op jit(solution)/shard_map/ppermute | solution.py:163
  152.6 24.2 %collective-permute-start.7 = (bf16[256,1024]{1,0:T(8,128)(2,1)}, bf16[256,1024]{1,0:T(8,128)(2,1)S(1)}, u32[]{:S(2)}, u32[]{:S(2)}) collective-permute-start(bf16[256,1024]{1,0:T(8,128)(2,1)} %shard_map.77), channel_id=1, source_target_pairs={{0,4},{2,6},{4,0},{6,2},{8,12},{10,14},{12,8},{14,10},{16,20},{18,... | collective-permute-start | bytes 1572872 | tf_op jit(solution)/shard_map/ppermute | solution.py:163
  152.9 24.0 %collective-permute-start.8 = (bf16[256,1024]{1,0:T(8,128)(2,1)}, bf16[256,1024]{1,0:T(8,128)(2,1)S(1)}, u32[]{:S(2)}, u32[]{:S(2)}) collective-permute-start(bf16[256,1024]{1,0:T(8,128)(2,1)} %shard_map.77), channel_id=1, source_target_pairs={{0,6},{2,0},{4,2},{6,4},{8,14},{10,8},{12,10},{14,12},{16,22},{18,... | collective-permute-start | bytes 1572872 | tf_op jit(solution)/shard_map/ppermute | solution.py:163
  176.9 0.8 copy-start.5
  177.7 0.9 copy-start.6
  185.2 4.3 %collective-permute-start.9 = (bf16[1024,1024]{1,0:T(8,128)(2,1)S(1)}, bf16[1024,1024]{1,0:T(8,128)(2,1)}, u32[]{:S(2)}, u32[]{:S(2)}) collective-permute-start(bf16[1024,1024]{1,0:T(8,128)(2,1)S(1)} %get-tuple-element.6), channel_id=1, source_target_pairs={{0,1},{1,0},{2,3},{3,2},{4,5},{5,4},{6,7},{7,6},{8,9},{9,8},{10,11... | collective-permute-start | bytes 6291464 | tf_op jit(solution)/shard_map/ppermute | solution.py:230
  192.7 4.7 %copy-start.7 = (bf16[2048,1024]{1,0:T(8,128)(2,1)S(1)}, bf16[2048,1024]{1,0:T(8,128)(2,1)}, u32[]{:S(2)}) copy-start(bf16[2048,1024]{1,0:T(8,128)(2,1)} %all-gather.2.cloned.1.call-done) | copy-start | bytes 12582916
  196.6 18.9 %collective-permute-start.11 = (bf16[256,1024]{1,0:T(8,128)(2,1)S(1)}, bf16[256,1024]{1,0:T(8,128)(2,1)S(1)}, u32[]{:S(2)}, u32[]{:S(2)}) collective-permute-start(bf16[256,1024]{1,0:T(8,128)(2,1)S(1)} %convolution_convert_fusion.2), channel_id=1, source_target_pairs={{0,4},{2,6},{4,0},{6,2},{8,12},{10,14},{12,8},{14,10},{16,20},{18,... | collective-permute-start | bytes 1572872 | tf_op jit(solution)/shard_map/ppermute | solution.py:163
  199.9 15.3 %collective-permute-start.10 = (bf16[256,1024]{1,0:T(8,128)(2,1)S(1)}, bf16[256,1024]{1,0:T(8,128)(2,1)S(1)}, u32[]{:S(2)}, u32[]{:S(2)}) collective-permute-start(bf16[256,1024]{1,0:T(8,128)(2,1)S(1)} %convolution_convert_fusion.3), channel_id=1, source_target_pairs={{0,6},{2,0},{4,2},{6,4},{8,14},{10,8},{12,10},{14,12},{16,22},{18,... | collective-permute-start | bytes 1572872 | tf_op jit(solution)/shard_map/ppermute | solution.py:163
  204.7 21.0 %collective-permute-start.12 = (bf16[256,1024]{1,0:T(8,128)(2,1)S(1)}, bf16[256,1024]{1,0:T(8,128)(2,1)S(1)}, u32[]{:S(2)}, u32[]{:S(2)}) collective-permute-start(bf16[256,1024]{1,0:T(8,128)(2,1)S(1)} %convolution_convert_fusion.1), channel_id=1, source_target_pairs={{0,2},{2,4},{4,6},{6,0},{8,10},{10,12},{12,14},{14,8},{16,18},{18,... | collective-permute-start | bytes 1572872 | tf_op jit(solution)/shard_map/ppermute | solution.py:163
  228.2 1.3 copy-start.2
Sparse Core Ops, SparseCore 0:
  50.5 81.9 all-gather.1
